TPU v7x, 32 devices: a whole 2x2x4 slice. The times are simulated.
32 devices in a mesh: pipe: 2 (over core), dp: 16 (over z, y, x).
Axes of the slice: x: 2, y: 2, z: 4, core: 2. Of those that a mesh axis runs over, the one named last changes fastest.
Arguments:
- page_inputs: bfloat16 [48, 20, 20, 512], P('dp', None, None, 'pipe'), may hold values from -6 to 6
- gain_one: bfloat16 [2, 512], P('pipe'), may hold values from 0.5 to 1.5
- bias_one: bfloat16 [2, 512], P('pipe'), may hold values from -3 to 3
- qkv_weight: bfloat16 [2, 512, 1536], P('pipe'), may hold values from -0.25 to 0.25
- query_bias: bfloat16 [2, 512], P('pipe'), may hold values from -3 to 3
- value_bias: bfloat16 [2, 512], P('pipe'), may hold values from -3 to 3
- bias_table: bfloat16 [2, 361, 16], P('pipe'), may hold values from -4 to 4
- proj_weight: bfloat16 [2, 512, 512], P('pipe'), may hold values from -0.75 to 0.75
- proj_bias: bfloat16 [2, 512], P('pipe'), may hold values from -3 to 3
- gain_two: bfloat16 [2, 512], P('pipe'), may hold values from 0.5 to 1.5
- bias_two: bfloat16 [2, 512], P('pipe'), may hold values from -3 to 3
- fc1_weight: bfloat16 [2, 512, 2048], P('pipe'), may hold values from -0.25 to 0.25
- fc1_bias: bfloat16 [2, 2048], P('pipe'), may hold values from -3 to 3
- fc2_weight: bfloat16 [2, 2048, 512], P('pipe'), may hold values from -0.125 to 0.125
- fc2_bias: bfloat16 [2, 512], P('pipe'), may hold values from -3 to 3
- merge_gain: bfloat16 [2048], replicated, may hold values from 0.5 to 1.5
- merge_bias: bfloat16 [2048], replicated, may hold values from -3 to 3
- merge_weight: bfloat16 [2048, 1024], P(None, 'pipe'), may hold values from -0.125 to 0.125
- cotangent: bfloat16 [48, 10, 10, 1024], P('dp', None, None, 'pipe'), may hold values from -6 to 6
Outputs:
- merged: bfloat16 [48, 10, 10, 1024], P('dp', None, None, 'pipe')
- grad_page_inputs: float32 [48, 20, 20, 512], P('dp', None, None, 'pipe')
- grad_gain_one: float32 [2, 512], P('pipe')
- grad_bias_one: float32 [2, 512], P('pipe')
- grad_qkv_weight: float32 [2, 512, 1536], P('pipe')
- grad_query_bias: float32 [2, 512], P('pipe')
- grad_value_bias: float32 [2, 512], P('pipe')
- grad_bias_table: float32 [2, 361, 16], P('pipe')
- grad_proj_weight: float32 [2, 512, 512], P('pipe')
- grad_proj_bias: float32 [2, 512], P('pipe')
- grad_gain_two: float32 [2, 512], P('pipe')
- grad_bias_two: float32 [2, 512], P('pipe')
- grad_fc1_weight: float32 [2, 512, 2048], P('pipe')
- grad_fc1_bias: float32 [2, 2048], P('pipe')
- grad_fc2_weight: float32 [2, 2048, 512], P('pipe')
- grad_fc2_bias: float32 [2, 512], P('pipe')
- grad_merge_gain: float32 [2048], replicated
- grad_merge_bias: float32 [2048], replicated
- grad_merge_weight: float32 [2048, 1024], P(None, 'pipe')
All inputs are finite; a program needn't handle non-finite values.
Results may differ from a plain program's by a relative error of at most 0.018.
Values may be sent and summed in bfloat16 or wider, within the bound.
A program may use at most 256 MiB of HBM per device.

v0:
```python
from functools import partial

import jax
import jax.numpy as jnp
from jax import lax
from jax.sharding import PartitionSpec as P

WINDOW = 10
PAGE_H = 20
PAGE_W = 20
PAGES_MB = 1


norm_eps = 1e-05
highest = lax.Precision.HIGHEST


def passed_along(value, axis, steps):
    count = lax.axis_size(axis)
    first, last = (max(0, -steps), min(count, count - steps))
    return lax.ppermute(value, axis, [(source, source + steps) for source in range(first, last)])


def from_partner(block, axis, stride):
    count = lax.axis_size(axis)
    route = []
    for low in range(count):
        high = low | 1 << stride
        if high != low and high < count:
            route += [(low, high), (high, low)]
    return lax.ppermute(block, axis, route)


def norm_forward(values, scale_gain, shift_bias):
    average = jnp.mean(values, axis=-1, keepdims=True)
    centred = values - average
    inv_std = lax.rsqrt(jnp.mean(centred * centred, axis=-1, keepdims=True) + norm_eps)
    unit_rows = centred * inv_std
    return (unit_rows * scale_gain + shift_bias, unit_rows, inv_std)


def norm_backward(grad_normed, unit_rows, inv_std, scale_gain):
    grad_unit = grad_normed * scale_gain
    return inv_std * (
        grad_unit
        - jnp.mean(grad_unit, axis=-1, keepdims=True)
        - unit_rows * jnp.mean(grad_unit * unit_rows, axis=-1, keepdims=True)
    )


def to_windows(spatial):
    page_count, grid_height, grid_width, channels = spatial.shape
    window_tiles = spatial.reshape(
        page_count, grid_height // WINDOW, WINDOW, grid_width // WINDOW, WINDOW, channels
    )
    return window_tiles.transpose(0, 1, 3, 2, 4, 5).reshape(-1, WINDOW * WINDOW, channels)


def from_windows(window_tiles, page_count):
    channels = window_tiles.shape[-1]
    spatial = window_tiles.reshape(
        page_count, PAGE_H // WINDOW, PAGE_W // WINDOW, WINDOW, WINDOW, channels
    )
    return spatial.transpose(0, 1, 3, 2, 4, 5).reshape(page_count, PAGE_H, PAGE_W, channels)


def relative_index():
    places = jnp.arange(WINDOW * WINDOW, dtype=jnp.int32)
    row_place = places // WINDOW
    col_place = places % WINDOW
    row_delta = row_place[:, None] - row_place[None, :] + WINDOW - 1
    col_delta = col_place[:, None] - col_place[None, :] + WINDOW - 1
    return row_delta * (2 * WINDOW - 1) + col_delta


def position_table():
    table_span = (2 * WINDOW - 1) ** 2
    rel_index = relative_index().reshape(-1)
    return (rel_index[:, None] == jnp.arange(table_span, dtype=jnp.int32)[None, :]).astype(
        jnp.float32
    )


def shift_mask():
    row_ids = jnp.arange(PAGE_H, dtype=jnp.int32)
    col_ids = jnp.arange(PAGE_W, dtype=jnp.int32)
    row_region = (row_ids >= PAGE_H - WINDOW).astype(jnp.int32) + (
        row_ids >= PAGE_H - WINDOW // 2
    ).astype(jnp.int32)
    col_region = (col_ids >= PAGE_W - WINDOW).astype(jnp.int32) + (
        col_ids >= PAGE_W - WINDOW // 2
    ).astype(jnp.int32)
    region = row_region[:, None] * 3 + col_region[None, :]
    region_tiles = to_windows(region[None, :, :, None])[:, :, 0]
    return jnp.where(region_tiles[:, :, None] != region_tiles[:, None, :], -100.0, 0.0).astype(
        jnp.float32
    )


def patch_merge(spatial):
    page_count, grid_height, grid_width, channels = spatial.shape
    quad_rows = spatial.reshape(page_count, grid_height // 2, 2, grid_width // 2, 2, channels)
    return quad_rows.transpose(0, 1, 3, 4, 2, 5).reshape(-1, 4 * channels)


def patch_split(merged_rows, page_count):
    channels = merged_rows.shape[-1] // 4
    quad_rows = merged_rows.reshape(page_count, PAGE_H // 2, PAGE_W // 2, 2, 2, channels)
    return quad_rows.transpose(0, 1, 4, 2, 3, 5).reshape(page_count, PAGE_H, PAGE_W, channels)


def roll_in(spatial, shift_flag):
    rolled = jnp.roll(spatial, (-(WINDOW // 2), -(WINDOW // 2)), axis=(1, 2))
    return jnp.where(shift_flag > 0, rolled, spatial)


def roll_out(spatial, shift_flag):
    rolled = jnp.roll(spatial, (WINDOW // 2, WINDOW // 2), axis=(1, 2))
    return jnp.where(shift_flag > 0, rolled, spatial)


def block_forward(spatial, weights, shift_flag, mask_windows, one_hot):
    (
        gain_one,
        bias_one,
        qkv_weight,
        query_bias,
        value_bias,
        bias_table,
        proj_weight,
        proj_bias,
        gain_two,
        bias_two,
        fc1_weight,
        fc1_bias,
        fc2_weight,
        fc2_bias,
    ) = weights
    page_count = spatial.shape[0]
    tokens = to_windows(roll_in(spatial, shift_flag))
    window_count, window_area, width_model = tokens.shape
    head_count = bias_table.shape[1]
    head_dim = width_model // head_count
    flat_rows = tokens.reshape(-1, width_model)
    normed_full, unit_one, inv_one = norm_forward(flat_rows, gain_one, bias_one)
    normed = normed_full.astype(jnp.bfloat16)
    projected = jnp.dot(normed, qkv_weight, preferred_element_type=jnp.float32)
    head_shape = (window_count, window_area, head_count, head_dim)
    queries = (projected[:, :width_model] + query_bias).astype(jnp.bfloat16).reshape(head_shape)
    key_rows = projected[:, width_model : 2 * width_model].astype(jnp.bfloat16).reshape(head_shape)
    value_rows = (
        (projected[:, 2 * width_model :] + value_bias).astype(jnp.bfloat16).reshape(head_shape)
    )
    position = (
        jnp.dot(one_hot, bias_table, precision=highest)
        .reshape(window_area, window_area, head_count)
        .transpose(2, 0, 1)
    )
    scores = (
        jnp.einsum("bqhc,bkhc->bhqk", queries, key_rows, preferred_element_type=jnp.float32)
        * head_dim ** (-0.5)
        + position[None]
    )
    scores = (
        scores.reshape(page_count, -1, head_count, window_area, window_area)
        + shift_flag * mask_windows[None, :, None]
    ).reshape(window_count, head_count, window_area, window_area)
    row_peak = jnp.max(scores, axis=-1, keepdims=True)
    exp_scores = jnp.exp(scores - row_peak)
    attention = exp_scores / jnp.sum(exp_scores, axis=-1, keepdims=True)
    attention_low = attention.astype(jnp.bfloat16)
    attended = jnp.einsum(
        "bhqk,bkhc->bqhc", attention_low, value_rows, preferred_element_type=jnp.float32
    )
    attended = attended.reshape(-1, width_model).astype(jnp.bfloat16)
    hidden = flat_rows + (
        jnp.dot(attended, proj_weight, preferred_element_type=jnp.float32) + proj_bias
    )
    normed_two_full, unit_two, inv_two = norm_forward(hidden, gain_two, bias_two)
    normed_two = normed_two_full.astype(jnp.bfloat16)
    pre_act = jnp.dot(normed_two, fc1_weight, preferred_element_type=jnp.float32) + fc1_bias
    activated = jax.nn.gelu(pre_act, approximate=False).astype(jnp.bfloat16)
    output = hidden + (
        jnp.dot(activated, fc2_weight, preferred_element_type=jnp.float32) + fc2_bias
    )
    spatial_out = roll_out(
        from_windows(output.reshape(window_count, window_area, width_model), page_count), shift_flag
    )
    saved_state = (
        normed,
        unit_one,
        inv_one,
        queries,
        key_rows,
        value_rows,
        attention,
        attention_low,
        attended,
        unit_two,
        inv_two,
        normed_two,
        pre_act,
        activated,
    )
    return (spatial_out, saved_state)


def block_backward(grad_spatial, saved_state, weights, shift_flag, one_hot):
    (
        gain_one,
        bias_one,
        qkv_weight,
        query_bias,
        value_bias,
        bias_table,
        proj_weight,
        proj_bias,
        gain_two,
        bias_two,
        fc1_weight,
        fc1_bias,
        fc2_weight,
        fc2_bias,
    ) = weights
    (
        normed,
        unit_one,
        inv_one,
        queries,
        key_rows,
        value_rows,
        attention,
        attention_low,
        attended,
        unit_two,
        inv_two,
        normed_two,
        pre_act,
        activated,
    ) = saved_state
    page_count = grad_spatial.shape[0]
    grad_tokens = to_windows(roll_in(grad_spatial, shift_flag))
    window_count, window_area, width_model = grad_tokens.shape
    head_count = bias_table.shape[1]
    head_dim = width_model // head_count
    grad_rows = grad_tokens.reshape(-1, width_model)
    grad_mlp = grad_rows.astype(jnp.bfloat16)
    grad_fc2_weight = jnp.einsum(
        "nf,nd->fd", activated, grad_mlp, preferred_element_type=jnp.float32
    )
    grad_fc2_bias = jnp.sum(grad_mlp, axis=0, dtype=jnp.float32)
    grad_activated = jnp.einsum(
        "nd,fd->nf", grad_mlp, fc2_weight, preferred_element_type=jnp.float32
    )
    gelu_exact = partial(jax.nn.gelu, approximate=False)
    grad_pre = jax.vjp(gelu_exact, pre_act)[1](grad_activated)[0].astype(jnp.bfloat16)
    grad_fc1_weight = jnp.einsum(
        "nd,nf->df", normed_two, grad_pre, preferred_element_type=jnp.float32
    )
    grad_fc1_bias = jnp.sum(grad_pre, axis=0, dtype=jnp.float32)
    grad_normed_two = jnp.einsum(
        "nf,df->nd", grad_pre, fc1_weight, preferred_element_type=jnp.float32
    )
    grad_gain_two = jnp.sum(grad_normed_two * unit_two, axis=0)
    grad_bias_two = jnp.sum(grad_normed_two, axis=0)
    grad_hidden = grad_rows + norm_backward(grad_normed_two, unit_two, inv_two, gain_two)
    grad_branch = grad_hidden.astype(jnp.bfloat16)
    grad_proj_weight = jnp.einsum(
        "nd,ne->de", attended, grad_branch, preferred_element_type=jnp.float32
    )
    grad_proj_bias = jnp.sum(grad_branch, axis=0, dtype=jnp.float32)
    grad_attended = jnp.einsum(
        "ne,de->nd", grad_branch, proj_weight, preferred_element_type=jnp.float32
    )
    grad_attended = grad_attended.astype(jnp.bfloat16).reshape(
        window_count, window_area, head_count, head_dim
    )
    grad_attention = jnp.einsum(
        "bqhc,bkhc->bhqk", grad_attended, value_rows, preferred_element_type=jnp.float32
    )
    grad_values = jnp.einsum(
        "bhqk,bqhc->bkhc", attention_low, grad_attended, preferred_element_type=jnp.float32
    ).astype(jnp.bfloat16)
    grad_scores = (
        attention * (grad_attention - jnp.sum(attention * grad_attention, axis=-1, keepdims=True))
    ).astype(jnp.bfloat16)
    scale_factor = head_dim ** (-0.5)
    grad_queries = (
        jnp.einsum("bhqk,bkhc->bqhc", grad_scores, key_rows, preferred_element_type=jnp.float32)
        * scale_factor
    ).astype(jnp.bfloat16)
    grad_keys = (
        jnp.einsum("bhqk,bqhc->bkhc", grad_scores, queries, preferred_element_type=jnp.float32)
        * scale_factor
    ).astype(jnp.bfloat16)
    score_sums = jnp.sum(grad_scores, axis=0, dtype=jnp.float32)
    score_sums = score_sums.transpose(1, 2, 0).reshape(window_area * window_area, head_count)
    grad_table = jnp.einsum("pt,ph->th", one_hot, score_sums, precision=highest)
    grad_query_rows = grad_queries.reshape(-1, width_model)
    grad_value_rows = grad_values.reshape(-1, width_model)
    grad_qkv = jnp.concatenate(
        [grad_query_rows, grad_keys.reshape(-1, width_model), grad_value_rows], axis=-1
    )
    grad_qkv_weight = jnp.einsum("nd,ne->de", normed, grad_qkv, preferred_element_type=jnp.float32)
    grad_query_bias = jnp.sum(grad_query_rows, axis=0, dtype=jnp.float32)
    grad_value_bias = jnp.sum(grad_value_rows, axis=0, dtype=jnp.float32)
    grad_normed = jnp.einsum("ne,de->nd", grad_qkv, qkv_weight, preferred_element_type=jnp.float32)
    grad_gain_one = jnp.sum(grad_normed * unit_one, axis=0)
    grad_bias_one = jnp.sum(grad_normed, axis=0)
    grad_flat = grad_hidden + norm_backward(grad_normed, unit_one, inv_one, gain_one)
    grad_input = roll_out(
        from_windows(grad_flat.reshape(window_count, window_area, width_model), page_count),
        shift_flag,
    )
    grad_terms = (
        grad_gain_one,
        grad_bias_one,
        grad_qkv_weight,
        grad_query_bias,
        grad_value_bias,
        grad_table,
        grad_proj_weight,
        grad_proj_bias,
        grad_gain_two,
        grad_bias_two,
        grad_fc1_weight,
        grad_fc1_bias,
        grad_fc2_weight,
        grad_fc2_bias,
    )
    return (grad_input, grad_terms)


def shards(
    page_inputs,
    gain_one,
    bias_one,
    qkv_weight,
    query_bias,
    value_bias,
    bias_table,
    proj_weight,
    proj_bias,
    gain_two,
    bias_two,
    fc1_weight,
    fc1_bias,
    fc2_weight,
    fc2_bias,
    merge_gain,
    merge_bias,
    merge_weight,
    cotangent,
):
    segment_index = lax.axis_index("pipe")
    is_first = segment_index == 0
    shift_flag = segment_index.astype(jnp.float32)
    weights = (
        gain_one[0].astype(jnp.float32),
        bias_one[0].astype(jnp.float32),
        qkv_weight[0],
        query_bias[0].astype(jnp.float32),
        value_bias[0].astype(jnp.float32),
        bias_table[0].astype(jnp.float32),
        proj_weight[0],
        proj_bias[0].astype(jnp.float32),
        gain_two[0].astype(jnp.float32),
        bias_two[0].astype(jnp.float32),
        fc1_weight[0],
        fc1_bias[0].astype(jnp.float32),
        fc2_weight[0],
        fc2_bias[0].astype(jnp.float32),
    )
    head_gain = merge_gain.astype(jnp.float32)
    head_bias = merge_bias.astype(jnp.float32)
    one_hot = position_table()
    mask_windows = shift_mask()
    micro_pages = PAGES_MB
    micro_count = page_inputs.shape[0] // micro_pages
    other_half = passed_along(page_inputs, "pipe", -1)
    full_inputs = jnp.concatenate([page_inputs, other_half], axis=-1)
    width_model = full_inputs.shape[-1]
    empty_pages = jnp.zeros((micro_pages, PAGE_H, PAGE_W, width_model), jnp.bfloat16)
    head_rows = micro_pages * (PAGE_H // 2) * (PAGE_W // 2)
    merge_in = 4 * width_model
    received = empty_pages
    kept_inputs = []
    kept_heads = []
    merged_parts = []
    for tick_index in range(micro_count + 1):
        if tick_index < micro_count:
            own_pages = full_inputs[tick_index * micro_pages : (tick_index + 1) * micro_pages]
        else:
            own_pages = empty_pages
        block_in = jnp.where(is_first, own_pages, received)
        block_out, unused = block_forward(
            block_in.astype(jnp.float32), weights, shift_flag, mask_windows, one_hot
        )
        head_normed = norm_forward(patch_merge(block_out), head_gain, head_bias)[0].astype(
            jnp.bfloat16
        )
        payload = jnp.where(
            is_first, block_out.astype(jnp.bfloat16).reshape(head_normed.shape), head_normed
        )
        arrived = from_partner(payload, "pipe", 0)
        received = arrived.reshape(empty_pages.shape)
        if tick_index < micro_count:
            kept_inputs.append(received)
        if tick_index >= 1:
            head_in = jnp.where(is_first, arrived, head_normed)
            kept_heads.append(head_in)
            merged_parts.append(
                jnp.dot(head_in, merge_weight, preferred_element_type=jnp.float32).astype(
                    jnp.bfloat16
                )
            )
    cot_flat = cotangent.reshape(-1, cotangent.shape[-1])
    grad_totals = tuple((jnp.zeros(weight_item.shape, jnp.float32) for weight_item in weights))
    grad_head_weight = jnp.zeros(merge_weight.shape, jnp.float32)
    grad_head_gain = jnp.zeros((merge_in,), jnp.float32)
    grad_head_bias = jnp.zeros((merge_in,), jnp.float32)
    grad_input_parts = []
    pending = empty_pages
    for tick_index in range(micro_count + 1):
        head_valid = tick_index < micro_count
        if head_valid:
            cot_rows = cot_flat[tick_index * head_rows : (tick_index + 1) * head_rows]
            grad_head_weight = grad_head_weight + jnp.einsum(
                "nc,no->co", kept_heads[tick_index], cot_rows, preferred_element_type=jnp.float32
            )
        if head_valid:
            partial_term = jnp.einsum(
                "no,co->nc", cot_rows, merge_weight, preferred_element_type=jnp.float32
            ).astype(jnp.bfloat16)
        else:
            partial_term = jnp.zeros((head_rows, merge_in), jnp.bfloat16)
        payload = jnp.where(is_first, partial_term, pending.reshape(partial_term.shape))
        arrived = from_partner(payload, "pipe", 0)
        head_grad = partial_term.astype(jnp.float32) + arrived.astype(jnp.float32)
        grad_from_next = arrived.reshape(empty_pages.shape).astype(jnp.float32)
        if tick_index >= 1:
            own_pages = full_inputs[(tick_index - 1) * micro_pages : tick_index * micro_pages]
        else:
            own_pages = empty_pages
        later_pages = kept_inputs[tick_index] if head_valid else empty_pages
        block_in = jnp.where(is_first, own_pages, later_pages)
        block_out, saved_state = block_forward(
            block_in.astype(jnp.float32), weights, shift_flag, mask_windows, one_hot
        )
        unused, head_unit, head_inv = norm_forward(patch_merge(block_out), head_gain, head_bias)
        grad_merge_rows = norm_backward(head_grad, head_unit, head_inv, head_gain)
        grad_out = jnp.where(is_first, grad_from_next, patch_split(grad_merge_rows, micro_pages))
        grad_input, grad_terms = block_backward(grad_out, saved_state, weights, shift_flag, one_hot)
        tick_valid = jnp.where(is_first, tick_index >= 1, head_valid).astype(jnp.float32)
        grad_totals = tuple(
            (total + tick_valid * term for total, term in zip(grad_totals, grad_terms))
        )
        if head_valid:
            grad_head_gain = grad_head_gain + shift_flag * jnp.sum(head_grad * head_unit, axis=0)
            grad_head_bias = grad_head_bias + shift_flag * jnp.sum(head_grad, axis=0)
        pending = grad_input.astype(jnp.bfloat16)
        if tick_index >= 1:
            grad_input_parts.append(grad_input)
    grad_inputs = jnp.concatenate(grad_input_parts, axis=0)
    half_width = width_model // 2
    other_grad = passed_along(grad_inputs[..., half_width:].astype(jnp.bfloat16), "pipe", 1).astype(
        jnp.float32
    )
    grad_page_inputs = jnp.where(is_first, grad_inputs[..., :half_width], other_grad)
    norm_sums = lax.psum((grad_head_gain, grad_head_bias), ("pipe", "dp"))
    summed_all = lax.psum(
        (
            grad_totals[0],
            grad_totals[1],
            grad_totals[2],
            grad_totals[3],
            grad_totals[4],
            grad_totals[5],
            grad_totals[6],
            grad_totals[7],
            grad_totals[8],
            grad_totals[9],
            grad_totals[10],
            grad_totals[11],
            grad_totals[12],
            grad_totals[13],
            grad_head_weight,
        ),
        "dp",
    )
    summed = summed_all[:14]
    weight_sum = summed_all[14]
    merged = jnp.concatenate(merged_parts, axis=0).reshape(
        micro_count * micro_pages, PAGE_H // 2, PAGE_W // 2, -1
    )
    return (
        merged,
        grad_page_inputs,
        summed[0][None],
        summed[1][None],
        summed[2][None],
        summed[3][None],
        summed[4][None],
        summed[5][None],
        summed[6][None],
        summed[7][None],
        summed[8][None],
        summed[9][None],
        summed[10][None],
        summed[11][None],
        summed[12][None],
        summed[13][None],
        norm_sums[0],
        norm_sums[1],
        weight_sum,
    )


def solution(mesh):
    in_specs = (
        P("dp", None, None, "pipe"),
        P("pipe", None),
        P("pipe", None),
        P("pipe", None, None),
        P("pipe", None),
        P("pipe", None),
        P("pipe", None, None),
        P("pipe", None, None),
        P("pipe", None),
        P("pipe", None),
        P("pipe", None),
        P("pipe", None, None),
        P("pipe", None),
        P("pipe", None, None),
        P("pipe", None),
        P(),
        P(),
        P(None, "pipe"),
        P("dp", None, None, "pipe"),
    )
    out_specs = (
        P("dp", None, None, "pipe"),
        P("dp", None, None, "pipe"),
        P("pipe", None),
        P("pipe", None),
        P("pipe", None, None),
        P("pipe", None),
        P("pipe", None),
        P("pipe", None, None),
        P("pipe", None, None),
        P("pipe", None),
        P("pipe", None),
        P("pipe", None),
        P("pipe", None, None),
        P("pipe", None),
        P("pipe", None, None),
        P("pipe", None),
        P(),
        P(),
        P(None, "pipe"),
    )
    return jax.shard_map(shards, mesh=mesh, in_specs=in_specs, out_specs=out_specs, check_vma=False)
```

profile of v0, /device:TPU:0, one launch (start us, length us, event | category | flops | bytes accessed | tf_op | source)
XLA Modules:
  0.0 1650.5 jit_solution(12467421337051972551)
XLA Ops:
  8.7 3.6 slice_reduce_fusion.1
  12.3 3.3 broadcast_select_fusion.20
  17.9 5.3 fusion.196
  55.1 3.9 add_convert_fusion.13
  81.4 5.7 fusion.792
  96.2 25.5 %fusion.264 = f32[400,512]{1,0:T(8,128)} fusion(f32[400,512]{1,0:T(8,128)} %copy-done.130, bf16[1,2048,512]{2,1,0:T(8,128)(2,1)} %param.32, bf16[1,512,2048]{2,1,0:T(8,128)(2,1)S(1)} %copy-done, f32[2048]{0:T(1024)S(1)} %bitcast.736, f32[512]{0:T(512)S(1)} %bitcast.750, f32[512]{0:T(512)S(1)} %bitcast.724, f32[512]{0:T(512)S(1)} %bitcast.695, ...), kind=kOutput, calls=%fused_computation.408 | convolution fusion | flops 1733222400 | bytes 5850240 | tf_op jit(solution)/shard_map/dot_general | solution.py:184
  127.7 3.5 fusion.790
  152.7 5.1 fusion.834
  165.9 10.0 multiply_convert_fusion.4
  235.0 3.8 add_convert_fusion.19
  259.8 5.1 fusion.798
  271.2 11.3 fusion.261
  288.5 3.5 fusion.784
  314.0 5.1 fusion.816
  327.1 10.0 multiply_convert_fusion.7
  371.1 3.3 convert_reduce_fusion.19
  383.6 6.5 convert_reduce_fusion.7
  399.2 3.5 multiply_reduce_fusion.3
  430.1 3.8 multiply_reduce_fusion.18
  442.9 3.3 fusion.463
  455.9 4.2 fusion.355
  464.4 4.5 convolution_multiply_fusion.1
  472.7 3.4 fusion.753
  500.1 4.0 add_convert_fusion.17
  533.9 5.7 fusion.804
  548.7 11.5 fusion.258
  584.9 5.7 fusion.822
  598.4 10.0 multiply_convert_fusion.6
  623.1 5.0 fusion.780
  659.5 3.3 convert_reduce_fusion.18
  673.2 6.3 convert_reduce_fusion.6
  688.6 3.5 multiply_reduce_fusion.2
  720.5 3.9 multiply_reduce_fusion.17
  733.7 3.4 fusion.461
  755.0 3.6 fusion.456
  759.0 4.3 convolution_add_fusion.1
  763.4 3.9 fusion.580
  768.7 3.4 fusion.754
  802.4 3.6 add_convert_fusion.15
  835.8 5.7 fusion.810
  850.6 11.7 fusion.255
  886.9 5.7 fusion.828
  900.5 10.1 multiply_convert_fusion.5
  925.3 4.6 fusion.774
  974.7 6.6 convert_reduce_fusion.5
  990.3 3.5 multiply_reduce_fusion.1
  1021.3 3.8 multiply_reduce_fusion.16
  1034.1 3.3 fusion.459
  1056.9 5.3 convolution_add_fusion
  1062.2 4.0 fusion.581
  1067.7 3.4 fusion.755
  1096.7 6.0 convert_reduce_fusion.4
  1109.1 3.5 multiply_reduce_fusion
  1139.5 8.2 add_bitcast_fusion.1
  1149.3 3.9 add_bitcast_fusion
  1157.8 3.8 add_add_fusion
  1172.1 7.2 fusion.13
  1186.9 44.5 %all-reduce = (f32[2048]{0:T(1024)}, f32[2048]{0:T(1024)}) all-reduce(f32[2048]{0:T(1024)S(1)} %get-tuple-element.352, f32[2048]{0:T(1024)S(1)} %get-tuple-element.351), channel_id=1, replica_groups=mesh['pipe'=2,'dp'=16] {'pipe','dp'}, use_global_device_ids=true, to_apply=%region_149.150 | all-reduce | flops 4096 | bytes 32768 | tf_op jit(solution)/shard_map/psum | solution.py:470
  1231.4 7.0 fusion.12
  1269.0 6.2 fusion.292
  1275.2 5.2 fusion.291
  1280.4 82.2 %all-reduce.1 = (f32[1,512]{1,0:T(1,128)}, f32[1,512]{1,0:T(1,128)}, f32[1,512]{1,0:T(1,128)}, f32[1,512]{1,0:T(1,128)}, f32[1,361,16]{1,2,0:T(8,128)}, /*index=...) all-reduce(f32[1,512]{1,0:T(1,128)S(1)} %bitcast.745, ...), channel_id=1, replica_groups=mesh['pipe'=2,'dp'=16] {'dp'}, use_global_device_ids=true, to_apply=%region_96.97 | all-reduce | flops 11920 | bytes 95360 | tf_op jit(solution)/shard_map/psum | solution.py:471
  1365.5 263.4 %all-reduce.5.cloned.1.call-done = (f32[1,512,1536]{2,1,0:T(8,128)}, f32[1,512,512]{2,1,0:T(8,128)}, f32[1,512,2048]{2,1,0:T(8,128)}, f32[1,2048,512]{2,1,0:T(8,128)}, f32[2048,512]{1,0:T(8,128)}) async-done(((f32[1,512,1536]{2,1,0:T(8,128)}, f32[1,512,512]{2,1,0:T(8,128)}, f32[1,512,2048]{2,1,0:T(8,128)}, f32[1,2048,512]{2,1,0:T(8,128)}, f32[2048,512]{1,0:T(8,128)}), (f32[1,512,1536]{2,1,0:T(8,128)}, ...) | async-done | bytes 16777232 | tf_op jit(solution)/shard_map/psum | solution.py:471
  1628.9 3.9 copy.1066
  (1282 shorter events, 901.1 us)
Async XLA Ops:
  7.2 89.0 %copy-start = (bf16[1,512,2048]{2,1,0:T(8,128)(2,1)S(1)}, bf16[1,512,2048]{2,1,0:T(8,128)(2,1)}, u32[]{:S(2)}) copy-start(bf16[1,512,2048]{2,1,0:T(8,128)(2,1)} %param.30) | copy-start | bytes 6291460
  7.2 10.5 copy-start.300
  7.2 1621.7 %all-reduce.5.cloned.1.call-start = ((), (), s32[]{:S(2)}) async-start(), calls=%async_computation | async-start | bytes 33554432 | tf_op jit(solution)/shard_map/psum | solution.py:471
  7.3 27.2 %collective-permute-start = (bf16[3,20,20,256]{3,2,1,0:T(8,128)(2,1)}, bf16[3,20,20,256]{3,2,1,0:T(8,128)(2,1)}, u32[]{:S(2)}, u32[]{:S(2)}) collective-permute-start(bf16[3,20,20,256]{3,2,1,0:T(8,128)(2,1)} %param.19), channel_id=1, source_target_pairs={{16,0},{17,1},{18,2},{19,3},{20,4},{21,5},{22,6},{23,7},{24,8},{25... | collective-permute-start | bytes 1843208 | tf_op jit(solution)/shard_map/ppermute | solution.py:21
  15.6 15.5 collective-permute-start.5
  23.3 140.7 %copy-start.182 = (f32[1,512]{1,0:T(1,128)}, f32[1,512]{1,0:T(1,128)S(1)}, u32[]{:S(2)}) copy-start(f32[1,512]{1,0:T(1,128)S(1)} %add.1348) | copy-start | bytes 6148
  24.8 210.2 %copy-start.180 = (f32[1,512]{1,0:T(1,128)}, f32[1,512]{1,0:T(1,128)S(1)}, u32[]{:S(2)}) copy-start(f32[1,512]{1,0:T(1,128)S(1)} %add.1345) | copy-start | bytes 6148
  24.8 210.2 %copy-start.168 = (f32[1,512]{1,0:T(1,128)}, f32[1,512]{1,0:T(1,128)S(1)}, u32[]{:S(2)}) copy-start(f32[1,512]{1,0:T(1,128)S(1)} %mul.1592) | copy-start | bytes 6148
  24.8 49.0 %copy-start.190 = (f32[1,512]{1,0:T(1,128)}, f32[1,512]{1,0:T(1,128)S(1)}, u32[]{:S(2)}) copy-start(f32[1,512]{1,0:T(1,128)S(1)} %add.1346) | copy-start | bytes 6148
  24.9 48.9 %copy-start.194 = (f32[1,512]{1,0:T(1,128)}, f32[1,512]{1,0:T(1,128)S(1)}, u32[]{:S(2)}) copy-start(f32[1,512]{1,0:T(1,128)S(1)} %add.1347) | copy-start | bytes 6148
  24.9 71.3 %copy-start.245 = (f32[1,2048]{1,0:T(1,128)}, f32[1,2048]{1,0:T(1,128)S(1)}, u32[]{:S(2)}) copy-start(f32[1,2048]{1,0:T(1,128)S(1)} %add.1350) | copy-start | bytes 24580
  24.9 71.2 %copy-start.277 = (f32[1,512]{1,0:T(1,128)}, f32[1,512]{1,0:T(1,128)S(1)}, u32[]{:S(2)}) copy-start(f32[1,512]{1,0:T(1,128)S(1)} %add.1351) | copy-start | bytes 6148
  25.0 71.2 %copy-start.228 = (f32[1,512]{1,0:T(1,128)}, f32[1,512]{1,0:T(1,128)S(1)}, u32[]{:S(2)}) copy-start(f32[1,512]{1,0:T(1,128)S(1)} %add.1349) | copy-start | bytes 6148
  25.0 140.9 %copy-start.188 = (f32[1,512]{1,0:T(1,128)}, f32[1,512]{1,0:T(1,128)S(1)}, u32[]{:S(2)}) copy-start(f32[1,512]{1,0:T(1,128)S(1)} %mul.1593) | copy-start | bytes 6148
  25.0 166.2 %copy-start.174 = (f32[2048]{0:T(1024)}, f32[2048]{0:T(1024)S(1)}, u32[]{:S(2)}) copy-start(f32[2048]{0:T(1024)S(1)} %convert_element_type.854) | copy-start | bytes 24580
  25.1 166.2 %copy-start.151 = (f32[2048]{0:T(1024)}, f32[2048]{0:T(1024)S(1)}, u32[]{:S(2)}) copy-start(f32[2048]{0:T(1024)S(1)} %convert_element_type.853) | copy-start | bytes 24580
  139.9 24.1 %copy-start.17 = (f32[400,512]{1,0:T(8,128)}, f32[400,512]{1,0:T(8,128)S(1)}, u32[]{:S(2)}) copy-start(f32[400,512]{1,0:T(8,128)S(1)} %reshape_reshape.92) | copy-start | bytes 2457604
  165.6 10.4 copy-start.34
  165.6 10.3 copy-start.208
  165.9 10.0 copy-start.221
  165.9 11.2 copy-start.278
  165.9 11.2 copy-start.296
  181.5 12.1 copy-start.91
  193.6 12.5 collective-permute-start.1
  195.8 9.6 copy-start.187
  231.3 7.5 copy-start.30
  239.9 8.8 copy-start.129
  288.5 8.3 copy-start.31
  326.8 10.3 copy-start.79
  326.8 65.1 %copy-start.223 = (f32[400]{0:T(512)}, f32[400]{0:T(512)S(1)}, u32[]{:S(2)}) copy-start(f32[400]{0:T(512)S(1)} %broadcast_multiply_fusion.35) | copy-start | bytes 4804
  327.1 10.0 copy-start.237
  327.1 11.1 copy-start.297
  346.1 8.5 copy-start.152
  417.5 12.7 copy-start.169
  442.9 7.7 copy-start.210
  453.4 11.0 copy-start.181
  455.9 20.2 %collective-permute-start.2 = (bf16[100,2048]{1,0:T(8,128)(2,1)}, bf16[100,2048]{1,0:T(8,128)(2,1)}, u32[]{:S(2)}, u32[]{:S(2)}) collective-permute-start(bf16[100,2048]{1,0:T(8,128)(2,1)} %get-tuple-element.217), channel_id=1, source_target_pairs={{0,16},{16,0},{1,17},{17,1},{2,18},{18,2},{3,19},{19,3},{4,20},{20... | collective-permute-start | bytes 1228808 | tf_op jit(solution)/shard_map/ppermute | solution.py:31
  472.1 165.1 %collective-permute-start.6 = (bf16[100,2048]{1,0:T(8,128)(2,1)}, bf16[100,2048]{1,0:T(8,128)(2,1)}, u32[]{:S(2)}, u32[]{:S(2)}) collective-permute-start(bf16[100,2048]{1,0:T(8,128)(2,1)} %get-tuple-element.296), channel_id=1, source_target_pairs={{0,16},{16,0},{1,17},{17,1},{2,18},{18,2},{3,19},{19,3},{4,20},{20... | collective-permute-start | bytes 1228808 | tf_op jit(solution)/shard_map/ppermute | solution.py:31
  598.2 10.3 copy-start.76
  598.4 11.2 copy-start.298
  746.9 25.3 %collective-permute-start.3 = (bf16[100,2048]{1,0:T(8,128)(2,1)}, bf16[100,2048]{1,0:T(8,128)(2,1)}, u32[]{:S(2)}, u32[]{:S(2)}) collective-permute-start(bf16[100,2048]{1,0:T(8,128)(2,1)} %get-tuple-element.211), channel_id=1, source_target_pairs={{0,16},{16,0},{1,17},{17,1},{2,18},{18,2},{3,19},{19,3},{4,20},{20... | collective-permute-start | bytes 1228808 | tf_op jit(solution)/shard_map/ppermute | solution.py:31
  758.5 180.4 %collective-permute-start.7 = (bf16[100,2048]{1,0:T(8,128)(2,1)}, bf16[100,2048]{1,0:T(8,128)(2,1)}, u32[]{:S(2)}, u32[]{:S(2)}) collective-permute-start(bf16[100,2048]{1,0:T(8,128)(2,1)} %get-tuple-element.307), channel_id=1, source_target_pairs={{0,16},{16,0},{1,17},{17,1},{2,18},{18,2},{3,19},{19,3},{4,20},{20... | collective-permute-start | bytes 1228808 | tf_op jit(solution)/shard_map/ppermute | solution.py:31
  900.2 10.4 copy-start.73
  900.5 82.6 %copy-start.235 = (f32[400]{0:T(512)}, f32[400]{0:T(512)S(1)}, u32[]{:S(2)}) copy-start(f32[400]{0:T(512)S(1)} %add_rsqrt_fusion.17) | copy-start | bytes 4804
  900.5 11.4 copy-start.299
  1047.2 109.0 %collective-permute-start.4 = (bf16[100,2048]{1,0:T(8,128)(2,1)}, bf16[100,2048]{1,0:T(8,128)(2,1)}, u32[]{:S(2)}, u32[]{:S(2)}) collective-permute-start(bf16[100,2048]{1,0:T(8,128)(2,1)} %get-tuple-element.203), channel_id=1, source_target_pairs={{0,16},{16,0},{1,17},{17,1},{2,18},{18,2},{3,19},{19,3},{4,20},{20... | collective-permute-start | bytes 1228808 | tf_op jit(solution)/shard_map/ppermute | solution.py:31
  1056.3 14.9 collective-permute-start.8
  1105.5 31.3 %copy-start.19 = (f32[400,512]{1,0:T(8,128)}, f32[400,512]{1,0:T(8,128)S(1)}, u32[]{:S(2)}) copy-start(f32[400,512]{1,0:T(8,128)S(1)} %get-tuple-element.176) | copy-start | bytes 2457604
  1123.9 12.9 copy-start.100
  1139.5 8.2 copy-start.7
  1139.5 8.2 copy-start.8
  1139.5 8.7 copy-start.9
  1139.5 9.2 copy-start.93
  1139.5 9.7 copy-start.149
  1162.5 68.9 %copy-start.198 = (s32[10000]{0:T(1024)}, s32[10000]{0:T(1024)S(1)}, u32[]{:S(2)}) copy-start(s32[10000]{0:T(1024)S(1)} %add.1307) | copy-start | bytes 120004
  1172.1 8.4 copy-start.3
  1172.1 8.4 copy-start.113
  1231.4 9.6 copy-start.4
  1231.4 9.6 copy-start.115
  1261.5 7.5 copy-start.199
  1262.5 100.1 %collective-permute-start.9 = (bf16[3,20,20,256]{3,2,1,0:T(8,128)(2,1)}, bf16[3,20,20,256]{3,2,1,0:T(8,128)(2,1)}, u32[]{:S(2)}, u32[]{:S(2)}) collective-permute-start(bf16[3,20,20,256]{3,2,1,0:T(8,128)(2,1)} %slice.788), channel_id=1, source_target_pairs={{0,16},{1,17},{2,18},{3,19},{4,20},{5,21},{6,22},{7,23},{8,24},{9,... | collective-permute-start | bytes 1843208 | tf_op jit(solution)/shard_map/ppermute | solution.py:21
  1266.3 8.9 copy-start.161
  1266.3 8.9 copy-start.307
  1266.3 8.9 copy-start.308
  (256 other events, 1177.0 us)
Sparse Core Ops, SparseCore 0:
  1161.7 467.1 all-reduce.4
where the time goes:
time: 1670 us; the launch traced here: 1650 us
  local copies, waits for them, and re-layouts  620 us (37%)
  matrix products  406 us (24%)
  waiting for transfers between devices  263 us (16%)
  other arithmetic  209 us (13%)
  blocking collectives  127 us (8%)
  between operations  18.5 us (1%)
    psum x1, waiting for transfers between devices, shards(): lax.psum((grad_totals[0], grad_totals[1], grad_totals[2], grad_totals[3],...  263 us
    psum x1, blocking collectives, shards(): lax.psum((grad_totals[0], grad_totals[1], grad_totals[2], grad_totals[3],...  82.2 us
    unnamed x639, local copies, waits for them, and re-layouts  76.2 us
    dot_general x8, matrix products, block_forward(): jnp.dot(activated, fc2_weight, preferred_element_type=jnp.float32)  66.7 us
    psum x1, blocking collectives, shards(): norm_sums = lax.psum((grad_head_gain, grad_head_bias), ('pipe', 'dp'))  44.5 us
    sub x8, matrix products, block_forward(): exp_scores = jnp.exp(scores - row_peak)  43.6 us
    dot_general x4, matrix products, block_forward(): jnp.dot(normed_two, fc1_weight, preferred_element_type=jnp.float32)  40 us
    reduce_sum x24, other arithmetic, norm_forward(): jnp.mean(centred * centred, axis=-1, keepdims=True) + norm_eps  34.1 us
  transfers between devices with their start and end apart: 11, of which 1 were waited for; matrix products, arithmetic and copies ran while one was open for 34% of the time, Pallas kernels for 0%

commit v1 on v0

v1 whole, which is shorter than its diff:
```python
import functools

import jax
import jax.numpy as jnp
import numpy as np
from jax import lax
from jax.experimental import pallas as pl
from jax.experimental.pallas import tpu as pltpu
from jax.sharding import PartitionSpec as P

BF = jnp.bfloat16
F32 = jnp.float32
WINDOW = 10
AREA = 100
PAGE = 20
WP = 112
HALO = 304
MROWS = 160
EPS = 1e-05
NEG = -1e30
ROW_TILE = 512


def mm(a, b):
    return lax.dot_general(a, b, (((1,), (0,)), ((), ())), preferred_element_type=F32)


def mm_nt(a, b):
    return lax.dot_general(a, b, (((1,), (1,)), ((), ())), preferred_element_type=F32)


def mm_tn(a, b):
    return lax.dot_general(a, b, (((0,), (0,)), ((), ())), preferred_element_type=F32)


def unit_norm(values):
    centred = values - jnp.mean(values, axis=-1, keepdims=True)
    inv_std = lax.rsqrt(jnp.mean(centred * centred, axis=-1, keepdims=True) + EPS)
    return centred * inv_std, inv_std


def unit_norm_back(grad_normed, unit_rows, inv_std, gain):
    grad_unit = grad_normed * gain
    return inv_std * (
        grad_unit
        - jnp.mean(grad_unit, axis=-1, keepdims=True)
        - unit_rows * jnp.mean(grad_unit * unit_rows, axis=-1, keepdims=True)
    )


def place_tables(pages):
    tokens = pages * 2 * WP
    halo = -(-pages * AREA // 16) * 16
    merged = -(-pages * 50 // 16) * 16
    send0 = np.zeros((halo, tokens), np.float32)
    own1 = np.zeros((tokens, tokens), np.float32)
    halo1 = np.zeros((tokens, halo), np.float32)
    own2 = np.zeros((4 * merged, tokens), np.float32)
    halo2 = np.zeros((4 * merged, halo), np.float32)

    def row0(p, r, col):
        return (p * 2 + col // WINDOW) * WP + r * WINDOW + col % WINDOW

    def row1(p, r, col):
        shifted = (col - 5) % PAGE
        return (p * 2 + shifted // WINDOW) * WP + r * WINDOW + shifted % WINDOW

    def rowh(p, r, col):
        return p * AREA + r * PAGE + col

    for p in range(pages):
        for col in range(PAGE):
            for r in range(5):
                send0[rowh(p, r, col), row0(p, r, col)] = 1
                own1[row1(p, r, col), row0(p, r + 5, col)] = 1
                halo1[row1(p, r + 5, col), rowh(p, r, col)] = 1
        for k in range(4):
            for m in range(5):
                for n in range(10):
                    row = k * merged + p * 50 + m * 10 + n
                    r, col = 2 * m + k % 2, 2 * n + k // 2
                    if r >= 5:
                        own2[row, row1(p, r - 5, col)] = 1
                    else:
                        halo2[row, rowh(p, r, col)] = 1
    return tuple(jnp.asarray(t, BF) for t in (send0, own1, halo1, own2, halo2))


def code_matrices():
    select = np.zeros((WP, 384), np.float32)
    back = np.zeros((184, WP), np.float32)
    for i in range(AREA):
        code = (i // WINDOW) * 19 + i % WINDOW
        select[i, code] = 1
        back[183 - code, i] = 1
    return jnp.asarray(select, BF), jnp.asarray(back, BF)


def expand_table(table, select, pos):
    for h in range(table.shape[0]):
        spread = pltpu.roll(jnp.broadcast_to(table[h : h + 1, :], (184, 384)), 208, 1, stride=1, stride_axis=0)
        rows = mm(select[:, 0:184], spread.astype(BF)).astype(BF)
        pos[h * WP : (h + 1) * WP, :] = mm_nt(rows, select[...]).astype(BF)


def reduce_table(score, select, back, out):
    for h in range(out.shape[0]):
        block = score[h * WP : (h + 1) * WP, :]
        high = block.astype(BF)
        low = (block - high.astype(F32)).astype(BF)
        codes = mm(back[...], mm(high, select[...]).astype(BF)) + mm(back[...], mm(low, select[...]).astype(BF))
        turned = pltpu.roll(codes, 0, 1, stride=1, stride_axis=0)
        out[h : h + 1, 0:384] = jnp.sum(turned, axis=0, keepdims=True)


class Copies:
    def __init__(self, sems):
        self.sems, self.used = sems, 0

    def start(self, source, target):
        copy = pltpu.make_async_copy(source, target, self.sems.at[self.used])
        self.used += 1
        copy.start()
        return copy

    def pick(self, mine, own, other, target):
        copy = pltpu.make_async_copy(own, target, self.sems.at[self.used])
        away = pltpu.make_async_copy(other, target, self.sems.at[self.used])
        self.used += 1

        @pl.when(mine)
        def _():
            copy.start()

        @pl.when(jnp.logical_not(mine))
        def _():
            away.start()

        return copy


def head_masks(kind):
    lane = lax.broadcasted_iota(jnp.int32, (1, 128), 1) // 32
    return [jnp.where(lane == h, 1.0, 0.0).astype(kind) for h in range(4)]


def stack_heads(block, masks):
    return jnp.concatenate([block * mask for mask in masks], axis=0)


def pick_heads(stacked, masks):
    total = stacked[0:WP] * masks[0]
    for h in range(1, 4):
        total = total + stacked[h * WP : (h + 1) * WP] * masks[h]
    return total


def block_forward(x_ref, small, weights, ready, pos, mask, bufs, n_ref, copies, outs):
    qkv, attn, attended, hidden, act, dgelu = bufs
    wqkv, wproj, wfc1, _ = weights
    tokens = x_ref.shape[0]
    sent = []
    unit_one, _ = unit_norm(x_ref[...].astype(F32))
    n_ref[...] = (unit_one * small[0:1] + small[1:2]).astype(BF)
    zero = jnp.zeros((1, 512), F32)
    bias = [small[2:3], zero, small[3:4]]
    ready[0].wait()
    for j in range(6):
        shift = bias[j // 2][:, (j % 2) * 256 : (j % 2) * 256 + 256]
        qkv[:, j * 256 : j * 256 + 256] = (
            mm(n_ref[...], wqkv[:, j * 256 : j * 256 + 256]) + shift
        ).astype(BF)
    sent.append(copies.start(qkv, outs[0]))
    low_masks, masks = head_masks(BF), head_masks(F32)

    def window(w, carry):
        rows = pl.ds(pl.multiple_of(w * WP, 16), WP)
        side = mask[w % 2]
        for blk in range(4):
            q = qkv[rows, blk * 128 : blk * 128 + 128]
            k = qkv[rows, 512 + blk * 128 : 512 + blk * 128 + 128]
            v = qkv[rows, 1024 + blk * 128 : 1024 + blk * 128 + 128]
            s = mm_nt(stack_heads(q, low_masks), k) * 32**-0.5
            s = s + pos[blk * 4 * WP : (blk + 1) * 4 * WP, :].astype(F32)
            s = (s.reshape(4, WP, WP) + side[None]).reshape(4 * WP, WP)
            e = jnp.exp(s - jnp.max(s, axis=-1, keepdims=True))
            a = (e * (1.0 / jnp.sum(e, axis=-1, keepdims=True))).astype(BF)
            attn[pl.ds(pl.multiple_of((w * 4 + blk) * 4 * WP, 16), 4 * WP), :] = a
            attended[rows, blk * 128 : blk * 128 + 128] = pick_heads(mm(a, v), masks).astype(BF)
        return carry

    lax.fori_loop(0, tokens // WP, window, 0)
    sent.append(copies.start(attn, outs[1]))
    sent.append(copies.start(attended, outs[2]))
    ready[1].wait()
    for j in range(2):
        cols = slice(j * 256, j * 256 + 256)
        hidden[:, cols] = x_ref[:, cols].astype(F32) + (mm(attended[...], wproj[:, cols]) + small[4:5, cols])
    sent.append(copies.start(hidden, outs[3]))
    unit_two, _ = unit_norm(hidden[...])
    n_ref[...] = (unit_two * small[5:6] + small[6:7]).astype(BF)
    ready[2].wait()
    for j in range(8):
        cols = slice(j * 256, j * 256 + 256)
        u = mm(n_ref[...], wfc1[:, cols]) + small[8 + j // 2 : 9 + j // 2, (j % 2) * 256 : (j % 2) * 256 + 256]
        cdf = 0.5 + 0.5 * lax.erf(u * (0.5**0.5))
        act[:, cols] = (u * cdf).astype(BF)
        dgelu[:, cols] = (cdf + u * (jnp.exp(u * u * -0.5) * ((2 * np.pi) ** -0.5))).astype(BF)
    sent.append(copies.start(act, outs[4]))
    sent.append(copies.start(dgelu, outs[5]))
    ready[3].wait()
    return sent


def layer_out(bufs, weights, small, out):
    hidden, act = bufs[3], bufs[4]
    for j in range(2):
        cols = slice(j * 256, j * 256 + 256)
        out[:, cols] = (hidden[:, cols] + (mm(act[...], weights[3][:, cols]) + small[7:8, cols])).astype(BF)


def forward0_kernel(x_ref, small, table, select, mask, send0, *refs):
    own, other, outs, out, halo = refs[0:4], refs[4:8], refs[8:14], refs[14], refs[15]
    weights, bufs, pos, n_ref, sems = refs[16:20], refs[20:26], refs[26], refs[27], refs[28]
    copies = Copies(sems)
    mine = lax.axis_index("pipe") == 0
    ready = [copies.pick(mine, a, b, w) for a, b, w in zip(own, other, weights)]
    expand_table(table, select, pos)
    sent = block_forward(x_ref, small, weights, ready, pos, mask, bufs, n_ref, copies, outs)
    layer_out(bufs, weights, small, out)
    halo[...] = mm(send0[...], out[...]).astype(BF)
    for copy in sent:
        copy.wait()


def forward1_kernel(prev, arrived, own1, halo1, small, table, select, mask, *refs):
    own, other, x_ref, outs, out, halo = refs[0:4], refs[4:8], refs[8], refs[9:15], refs[15], refs[16]
    weights, bufs, pos, n_ref, sems = refs[17:21], refs[21:27], refs[27], refs[28], refs[29]
    copies = Copies(sems)
    mine = lax.axis_index("pipe") == 1
    ready = [copies.pick(mine, a, b, w) for a, b, w in zip(own, other, weights)]
    expand_table(table, select, pos)
    x_ref[...] = (mm(own1[...], prev[...]) + mm(halo1[...], arrived[...])).astype(BF)
    sent = block_forward(x_ref, small, weights, ready, pos, mask, bufs, n_ref, copies, outs)
    layer_out(bufs, weights, small, out)
    halo[...] = mm_tn(halo1[...], out[...]).astype(BF)
    for copy in sent:
        copy.wait()


def merge_kernel(own, arrived, own2, halo2, vectors, cot, wm_own, wm_other, merged, parts, grad_small, grad_own, grad_halo,
                 rows_ref, normed, ghead, wm, grad_w, sems):
    copies = Copies(sems)
    mine = lax.axis_index("pipe") == 0
    ready = [copies.pick(mine, wm_own, wm_other, wm.at[0]), copies.pick(mine, wm_other, wm_own, wm.at[1])]
    sent = []
    count = rows_ref.shape[0]
    for k in range(4):
        part = mm(own2[k * count : (k + 1) * count, :], own[...]) + mm(halo2[k * count : (k + 1) * count, :], arrived[...])
        rows_ref[:, k * 512 : k * 512 + 512] = part
    unit, inv_std = unit_norm(rows_ref[...])
    gain = vectors[0:1]
    normed[...] = (unit * gain + vectors[1:2]).astype(BF)
    for half in range(2):
        ready[half].wait()
        merged[half] = mm(normed[...], wm[half]).astype(BF)
        for k in range(4):
            cols = slice(k * 512, k * 512 + 512)
            term = mm_nt(cot[half], wm[half, cols, :]).astype(BF).astype(F32)
            if half == 0:
                ghead[:, cols] = term
            else:
                ghead[:, cols] = ghead[:, cols] + term
            grad_w[half, cols, :] = mm_tn(normed[:, cols], cot[half]).astype(BF)
        sent.append(copies.start(grad_w.at[half], parts.at[half, 6144:8192]))
    grad = ghead[...]
    over_rows = [jnp.sum(grad * unit, axis=0, keepdims=True), jnp.sum(grad, axis=0, keepdims=True)]
    for i in range(2):
        for k in range(4):
            grad_small[i * 4 + k : i * 4 + k + 1] = over_rows[i][:, k * 512 : k * 512 + 512]
    grad_rows = unit_norm_back(grad, unit, inv_std, gain).astype(BF)
    stacked = jnp.concatenate([grad_rows[:, k * 512 : k * 512 + 512] for k in range(4)], axis=0)
    grad_own[...] = mm_tn(own2[...], stacked)
    grad_halo[...] = mm_tn(halo2[...], stacked).astype(BF)
    for copy in sent:
        copy.wait()


def block_backward(layer, g_ref, x_ref, small, select, back, merge_sums, sources, mine, own, other, parts, refs):
    weights, bufs, gm, gpre, n_ref, dqkv, work, score_sum, grad_small, grad_w, tail, sems = refs
    wqkv, wproj, wfc1, wfc2 = weights
    qkv, attn, attended, hidden, act, dgelu = bufs
    copies = Copies(sems)
    got = {}

    def fetch(name, source, target):
        got[name] = copies.start(source, target)

    def fetch_weight(name, i):
        got[name] = copies.pick(mine, own[i], other[i], weights[i])

    fetch("act", sources[4], act)
    fetch_weight("fc2", 3)
    fetch("dgelu", sources[5], dgelu)
    fetch("hidden", sources[3], hidden)
    fetch_weight("fc1", 2)
    fetch("attended", sources[2], attended)
    fetch_weight("proj", 1)
    fetch("qkv", sources[0], qkv)
    fetch("attn", sources[1], attn)
    fetch_weight("wqkv", 0)
    tokens = g_ref.shape[0]
    sent = []

    def send(start, stop):
        sent.append(copies.start(grad_w.at[start:stop], parts.at[layer, start:stop]))

    def put(row, value):
        grad_small[row : row + 1] = jnp.sum(value, axis=0, keepdims=True)

    grad_small[...] = jnp.zeros_like(grad_small)
    gm[...] = g_ref[...].astype(BF)
    put(7, gm[...].astype(F32))
    got["act"].wait()
    got["fc2"].wait()
    got["dgelu"].wait()
    for j in range(8):
        cols = slice(j * 256, j * 256 + 256)
        grad_w[4096 + j * 256 : 4096 + j * 256 + 256, :] = mm_tn(act[:, cols], gm[...]).astype(BF)
        d = mm_nt(gm[...], wfc2[cols, :]) * dgelu[:, cols].astype(F32)
        low = d.astype(BF)
        gpre[:, cols] = low
        grad_small[8 + j // 2 : 9 + j // 2, (j % 2) * 256 : (j % 2) * 256 + 256] = jnp.sum(
            low.astype(F32), axis=0, keepdims=True
        )
    send(4096, 6144)
    got["hidden"].wait()
    unit, inv_std = unit_norm(hidden[...])
    n_ref[...] = (unit * small[5:6] + small[6:7]).astype(BF)
    for b in range(4):
        grad_w[2048 + b * 512 : 2048 + b * 512 + 512, :] = mm_tn(n_ref[...], gpre[:, b * 512 : b * 512 + 512]).astype(BF)
    send(2048, 4096)
    got["fc1"].wait()
    for j in range(2):
        work[:, j * 256 : j * 256 + 256] = mm_nt(gpre[...], wfc1[j * 256 : j * 256 + 256, :])
    dn = work[...]
    put(5, dn * unit)
    put(6, dn)
    g_ref[...] = g_ref[...] + unit_norm_back(dn, unit, inv_std, small[5:6])
    gm[...] = g_ref[...].astype(BF)
    put(4, gm[...].astype(F32))
    got["attended"].wait()
    grad_w[1536:2048, :] = mm_tn(attended[...], gm[...]).astype(BF)
    send(1536, 2048)
    got["proj"].wait()
    for j in range(2):
        n_ref[:, j * 256 : j * 256 + 256] = mm_nt(gm[...], wproj[j * 256 : j * 256 + 256, :]).astype(BF)
    low_masks, masks = head_masks(BF), head_masks(F32)
    score_sum[...] = jnp.zeros_like(score_sum)
    got["qkv"].wait()
    got["attn"].wait()

    def window(w, carry):
        rows = pl.ds(pl.multiple_of(w * WP, 16), WP)
        for blk in range(4):
            q = qkv[rows, blk * 128 : blk * 128 + 128]
            k = qkv[rows, 512 + blk * 128 : 512 + blk * 128 + 128]
            v = qkv[rows, 1024 + blk * 128 : 1024 + blk * 128 + 128]
            go = stack_heads(n_ref[rows, blk * 128 : blk * 128 + 128], low_masks)
            a = attn[pl.ds(pl.multiple_of((w * 4 + blk) * 4 * WP, 16), 4 * WP), :]
            p = mm_nt(go, v)
            wide = a.astype(F32)
            ap = wide * p
            ds = ap - wide * jnp.sum(ap, axis=-1, keepdims=True)
            low = ds.astype(BF)
            score_sum[blk * 4 * WP : (blk + 1) * 4 * WP, :] += low.astype(F32)
            dqkv[rows, 1024 + blk * 128 : 1024 + blk * 128 + 128] = mm_tn(a, go).astype(BF)
            dqkv[rows, blk * 128 : blk * 128 + 128] = (pick_heads(mm(low, k), masks) * 32**-0.5).astype(BF)
            dqkv[rows, 512 + blk * 128 : 512 + blk * 128 + 128] = (
                mm_tn(low, stack_heads(q, low_masks)) * 32**-0.5
            ).astype(BF)
        return carry

    lax.fori_loop(0, tokens // WP, window, 0)
    unit, inv_std = unit_norm(x_ref[...].astype(F32))
    n_ref[...] = (unit * small[0:1] + small[1:2]).astype(BF)
    for b in range(3):
        grad_w[b * 512 : b * 512 + 512, :] = mm_tn(n_ref[...], dqkv[:, b * 512 : b * 512 + 512]).astype(BF)
    send(0, 1536)
    put(2, dqkv[:, 0:512].astype(F32))
    put(3, dqkv[:, 1024:1536].astype(F32))
    got["wqkv"].wait()
    for j in range(2):
        work[:, j * 256 : j * 256 + 256] = mm_nt(dqkv[...], wqkv[j * 256 : j * 256 + 256, :])
    dn = work[...]
    put(0, dn * unit)
    put(1, dn)
    reduce_table(score_sum, select, back, grad_small.at[16:32])
    grad_small[32:40] = merge_sums[...]
    tail[...] = jnp.zeros_like(tail)
    tail[0:48] = grad_small[...].astype(BF)
    sent.append(copies.start(tail, parts.at[layer, 8192:]))
    g_ref[...] = g_ref[...] + unit_norm_back(dn, unit, inv_std, small[0:1])
    return sent


def backward1_kernel(grad_own, arrived, own1, halo1, x_ref, small, select, back, merge_sums, *refs):
    sources, own, other, _, parts, grad_prev, grad_halo, g_ref = refs[0:6], refs[6:10], refs[10:14], refs[14], *refs[15:19]
    rest = refs[19:]
    gm = rest[10]
    g_ref[...] = grad_own[...] + mm(halo1[...], arrived[...])
    mine = lax.axis_index("pipe") == 1
    sent = block_backward(1, g_ref, x_ref, small, select, back, merge_sums, sources, mine, own, other, parts,
                          (rest[0:4], rest[4:10], *rest[10:]))
    gm[...] = g_ref[...].astype(BF)
    grad_prev[...] = mm_tn(own1[...], gm[...])
    grad_halo[...] = mm_tn(halo1[...], gm[...]).astype(BF)
    for copy in sent:
        copy.wait()


def backward0_kernel(grad_own, arrived, send0, x_ref, small, select, back, merge_sums, *refs):
    sources, own, other, _, parts, g_ref = refs[0:6], refs[6:10], refs[10:14], refs[14], *refs[15:17]
    rest = refs[17:]
    g_ref[...] = grad_own[...] + mm_tn(send0[...], arrived[...])
    mine = lax.axis_index("pipe") == 0
    sent = block_backward(0, g_ref, x_ref, small, select, back, merge_sums, sources, mine, own, other, parts,
                          (rest[0:4], rest[4:10], *rest[10:]))
    for copy in sent:
        copy.wait()


def widen_kernel(total, wqkv, wproj, wfc1, wfc2, wmerge, tail, rows, stage, load_sem, store_sem):
    blocks = []
    for b in range(3):
        blocks.append((b * 512, wqkv.at[:, b * 512 : b * 512 + 512]))
    blocks.append((1536, wproj))
    for b in range(4):
        blocks.append((2048 + b * 512, wfc1.at[:, b * 512 : b * 512 + 512]))
    for b in range(4):
        blocks.append((4096 + b * 512, wfc2.at[b * 512 : b * 512 + 512, :]))
    for b in range(4):
        blocks.append((6144 + b * 512, wmerge.at[b * 512 : b * 512 + 512, :]))
    loads = []
    for i, (start, _) in enumerate(blocks + [(8192, None)]):
        count = min(512, total.shape[0] - start)
        copy = pltpu.make_async_copy(total.at[start : start + count], rows.at[start : start + count], load_sem.at[i])
        copy.start()
        loads.append(copy)
    stores = []
    for i, (start, target) in enumerate(blocks):
        slot = i % 4
        loads[i].wait()
        if i >= 4:
            stores[i - 4].wait()
        stage[slot] = rows[start : start + 512, :].astype(F32)
        copy = pltpu.make_async_copy(stage.at[slot], target, store_sem.at[slot])
        copy.start()
        stores.append(copy)
    loads[-1].wait()
    tail[...] = rows[8192:8240, :].astype(F32)
    for copy in stores[-4:]:
        copy.wait()


HBM = pl.BlockSpec(memory_space=pl.ANY)
VMEM = pl.BlockSpec(memory_space=pltpu.VMEM)


def call(kernel, args, outs, scratch, name, aliases=None):
    return pl.pallas_call(
        kernel,
        out_shape=[jax.ShapeDtypeStruct(s, d) for s, d, _ in outs],
        in_specs=[spec for _, spec in args],
        out_specs=[spec for _, _, spec in outs],
        scratch_shapes=[pltpu.SemaphoreType.DMA((s,)) if isinstance(s, int) else pltpu.VMEM(*s) for s in scratch],
        compiler_params=pltpu.CompilerParams(vmem_limit_bytes=60 * 1024 * 1024),
        input_output_aliases=aliases or {},
        name=name,
    )(*[value for value, _ in args])


def other_core(value):
    return lax.ppermute(value, "pipe", [(0, 1), (1, 0)])


def shift_masks(core):
    place = jnp.arange(WP, dtype=jnp.int32)
    pad = jnp.where(place < AREA, 0.0, NEG).astype(F32)
    row_late = ((place // WINDOW) >= 5) & (core == 1)
    masks = []
    for side in range(2):
        late = row_late.astype(jnp.int32) * 2 + (((place % WINDOW) >= 5) & (side == 1)).astype(jnp.int32)
        masks.append(jnp.where(late[:, None] != late[None, :], -100.0, 0.0).astype(F32) + pad[None, :])
    plain = jnp.broadcast_to(pad[None, None, :], (2, WP, WP))
    return plain, jnp.stack(masks)


MESH = pl.DeviceIdType.MESH
ORDERS = ((0, 1, 2), (1, 0, 2), (2, 0, 1))


def dp_axes(dp):
    bits=dp.bit_length()-1
    b0=bits//3; b1=(bits-b0)//2; b2=bits-b0-b1
    sizes=[1<<b0,1<<b1,1<<b2]
    return [(1,sizes[0]),(sizes[0],sizes[1]),(sizes[0]*sizes[1],sizes[2])]

ORDERS=((0,1,2),(1,0,2),(2,0,1))

class Line:
    def __init__(self, me, stride, size):
        self.size=size; self.pos=lax.rem(me // stride, size); self.up=me+stride; self.down=me-stride

def plan(dp, chunk):
    axes=dp_axes(dp); plans=[]; most=0
    for order in ORDERS:
        events=[]; length=chunk; slot=0
        for k,a in enumerate(order):
            n=axes[a][1]; piece=length//n
            for s in range(1,n):
                events.append(("rs",k,s,piece,slot)); slot+=2*piece if n>2 else piece
            length=piece
        for k in (2,1,0):
            a=order[k]; n=axes[a][1]
            piece=length
            for s in range(1,n):
                events.append(("ag",k,s,piece,0))
            length*=n
        plans.append(events); most=max(most,slot)
    return axes,plans,most

def comm_kernel(dp, nchunk, chunk, parts, out_hbm, acc, paired, slots, pair_send, pair_recv, load_sem, store_sem, send_sem, recv_sem):
    core=lax.axis_index("pipe"); me=lax.axis_index("dp")
    axes,plans,slot_rows=plan(dp,chunk)
    lines=[Line(me,st,n) for st,n in axes]
    partner=1-core
    barrier=pltpu.get_barrier_semaphore()
    pl.semaphore_signal(barrier,inc=1,device_id=(partner,me),device_id_type=MESH)
    expect=jnp.int32(1)
    for ln in lines:
        @pl.when(ln.pos>0)
        def _(): pl.semaphore_signal(barrier,inc=1,device_id=(core,ln.down),device_id_type=MESH)
        @pl.when(ln.pos<ln.size-1)
        def _(): pl.semaphore_signal(barrier,inc=1,device_id=(core,ln.up),device_id_type=MESH)
        expect=expect+jnp.where(ln.pos>0,1,0)+jnp.where(ln.pos<ln.size-1,1,0)
    pl.semaphore_wait(barrier,expect)

    def rows(start,count): return pl.ds(pl.multiple_of(start,16),count)
    def pair_copy(q):
        r=rows(q*chunk,chunk)
        return pltpu.make_async_remote_copy(src_ref=parts.at[partner, r],dst_ref=paired.at[r],send_sem=pair_send.at[q],recv_sem=pair_recv.at[q],device_id=(partner,me),device_id_type=MESH)
    def load(q):
        r=rows(q*chunk,chunk)
        return pltpu.make_async_copy(parts.at[core, r],acc.at[r],load_sem.at[q])
    def store(q):
        r=rows(q*chunk,chunk)
        return pltpu.make_async_copy(paired.at[r],out_hbm.at[r],store_sem.at[q])
    def begin(q,c):
        pair_copy(q).start(); load(q).start(); return c
    lax.fori_loop(0,nchunk,begin,0)

    def moves(q,kind,e):
        order=ORDERS[kind]; what,k,s,piece,slot=plans[kind][e]
        base=q*chunk; length=chunk
        for i in range(k):
            ln=lines[order[i]]; length=length//ln.size; base=base+ln.pos*length
        ln=lines[order[k]]; n=ln.size; p=ln.pos
        result=[]
        for d in range(2):
            ahead=ln.up if d==0 else ln.down
            mirrored=p if d==0 else n-1-p
            if what=="rs":
                sends=mirrored<=s-1; gets=jnp.logical_and(mirrored>=1,mirrored<=s)
                piece_of=p+n-s if d==0 else p-n+s
                piece_of=jnp.clip(piece_of,0,n-1)
                source=rows(base+piece_of*piece,piece)
                place=slot+(d*piece if n>2 else 0)
                target=rows(q*slot_rows+place,piece)
                next_of=p+n-s-1 if d==0 else p-n+s+1
                into=rows(base+jnp.clip(next_of,0,n-1)*piece,piece)
                copy=pltpu.make_async_remote_copy(src_ref=acc.at[source],dst_ref=slots.at[target],send_sem=send_sem.at[q,e,d],recv_sem=recv_sem.at[q,e,d],device_id=(core,ahead),device_id_type=MESH)
                result.append((sends,gets,copy,target,into))
            else:
                sends=jnp.logical_and(mirrored<n-1,mirrored>=s-1); gets=mirrored>=s
                piece_of=p-s+1 if d==0 else p+s-1
                source=rows(base+jnp.clip(piece_of,0,n-1)*piece,piece)
                copy=pltpu.make_async_remote_copy(src_ref=paired.at[source],dst_ref=paired.at[source],send_sem=send_sem.at[q,e,d],recv_sem=recv_sem.at[q,e,d],device_id=(core,ahead),device_id_type=MESH)
                result.append((sends,gets,copy,None,None))
        return result

    def finish(q,kind,e):
        for sends,gets,copy,target,into in moves(q,kind,e):
            @pl.when(gets)
            def _():
                copy.wait_recv()
                if into is not None:
                    acc[into,:]=(acc[into,:].astype(F32)+slots[target,:].astype(F32)).astype(BF)
            @pl.when(sends)
            def _():
                copy.wait_send()
    def event(q,kind,e):
        events=plans[kind]
        if e==0:
            load(q).wait(); pair_copy(q).wait()
            def add(i,c):
                r=rows(q*chunk+i*64,64)
                acc[r,:]=(acc[r,:].astype(F32)+paired[r,:].astype(F32)).astype(BF)
                return c
            lax.fori_loop(0,chunk//64,add,0)
        else:
            finish(q,kind,e-1)
        if e<len(events):
            if events[e][0]=="ag" and events[e-1][0]=="rs":
                base=q*chunk; length=chunk
                for a in ORDERS[kind]:
                    ln=lines[a]; length=length//ln.size; base=base+ln.pos*length
                r=rows(base,length)
                paired[r,:]=acc[r,:]
            for sends,gets,copy,target,into in moves(q,kind,e):
                @pl.when(sends)
                def _(): copy.start()
        else:
            store(q).start()
    count=len(plans[0])+1
    groups=-(-nchunk//3)
    def tick(t,c):
        for e in reversed(range(count)):
            j=t-e
            for kind in range(3):
                q=j*3+kind
                @pl.when(jnp.logical_and(j>=0,q<nchunk))
                def _(): event(q,kind,e)
        return c
    lax.fori_loop(0,groups+(count-1),tick,0)
    def end(q,c):
        store(q).wait(); return c
    lax.fori_loop(0,nchunk,end,0)

def sum_rows(parts, dp, chunk):
    rows = parts.shape[1]
    count = rows // chunk
    _, plans, slot_rows = plan(dp, chunk)
    events = len(plans[0])
    dma = pltpu.SemaphoreType.DMA
    return pl.pallas_call(
        functools.partial(comm_kernel, dp, count, chunk),
        out_shape=jax.ShapeDtypeStruct((rows, 512), BF),
        in_specs=[HBM],
        out_specs=HBM,
        scratch_shapes=[pltpu.VMEM((rows, 512), BF), pltpu.VMEM((rows, 512), BF), pltpu.VMEM((count * slot_rows, 512), BF),
                        dma((count,)), dma((count,)), dma((count,)), dma((count,)),
                        dma((count, events, 2)), dma((count, events, 2))],
        compiler_params=pltpu.CompilerParams(collective_id=0, has_side_effects=True, vmem_limit_bytes=60 * 1024 * 1024),
        name="sum_rows",
    )(parts)


def shards(
    page_inputs, gain_one, bias_one, qkv_weight, query_bias, value_bias, bias_table, proj_weight, proj_bias,
    gain_two, bias_two, fc1_weight, fc1_bias, fc2_weight, fc2_bias, merge_gain, merge_bias, merge_weight, cotangent,
):
    dp = lax.axis_size("dp")
    core = lax.axis_index("pipe")
    pages = page_inputs.shape[0]
    tokens = pages * 2 * WP
    heads = bias_table.shape[2]
    table = bias_table.shape[1]
    send0, own1, halo1, own2, halo2 = place_tables(pages)
    halo_rows, merged_rows = send0.shape[0], own2.shape[0] // 4

    def both(own):
        other = other_core(own)
        return [jnp.where(core == 0, own, other), jnp.where(core == 0, other, own)]

    mine = lax.dynamic_slice_in_dim(page_inputs, core * 10, 10, axis=1)
    yours = lax.dynamic_slice_in_dim(page_inputs, (1 - core) * 10, 10, axis=1)
    yours = other_core(yours)
    rows = jnp.concatenate([jnp.where(core == 0, mine, yours), jnp.where(core == 0, yours, mine)], axis=-1)
    rows = rows.reshape(pages, 10, 2, 10, 512).transpose(0, 2, 1, 3, 4).reshape(pages * 2, AREA, 512)
    x0 = jnp.pad(rows, ((0, 0), (0, WP - AREA), (0, 0))).reshape(tokens, 512)

    small_own = jnp.concatenate(
        [gain_one, bias_one, query_bias, value_bias, proj_bias, gain_two, bias_two, fc2_bias,
         fc1_bias.reshape(4, 512), jnp.zeros((4, 512), BF)], axis=0)
    small = [s.astype(F32) for s in both(small_own)]
    turned = jnp.pad(bias_table[0].T[:, ::-1], ((0, 0), (0, 384 - table)))
    tables = [t.astype(F32) for t in both(jnp.roll(turned, -4, axis=1))]
    select, back = code_matrices()
    masks = shift_masks(core)
    own = [qkv_weight[0], proj_weight[0], fc1_weight[0], fc2_weight[0]]
    other = [other_core(w) for w in own]
    wm_other = other_core(merge_weight)
    stacks = [(w, HBM) for w in own + other]

    cmine = lax.dynamic_slice_in_dim(cotangent, core * 5, 5, axis=1)
    cyours = other_core(lax.dynamic_slice_in_dim(cotangent, (1 - core) * 5, 5, axis=1))
    cot = jnp.stack([jnp.where(core == 0, cmine, cyours), jnp.where(core == 0, cyours, cmine)])
    cot = jnp.pad(cot.reshape(2, pages * 50, 512), ((0, 0), (0, merged_rows - pages * 50), (0, 0)))

    def at(spec, *values):
        return [(v, spec) for v in values]

    saved_shapes = [((tokens, 1536), BF), ((pages * 2 * heads * WP, WP), BF), ((tokens, 512), BF), ((tokens, 512), F32),
                    ((tokens, 2048), BF), ((tokens, 2048), BF)]
    saved_out = [(*shape, HBM) for shape in saved_shapes]
    weight_shapes = [(w.shape, BF) for w in own]
    rows = ((tokens, 512), BF)
    wide_rows = ((tokens, 512), F32)
    halo = ((halo_rows, 512), BF)
    scratch = weight_shapes + saved_shapes + [((heads * WP, WP), BF), rows, 10]
    *saved0, out0, send = call(
        forward0_kernel, at(VMEM, x0, small[0], tables[0], select, masks[0], send0) + stacks,
        saved_out + [(*rows, VMEM), (*halo, VMEM)], scratch, "layer_zero")
    arrived = other_core(send)
    x1, *saved1, out1, send = call(
        forward1_kernel, at(VMEM, out0, arrived, own1, halo1, small[1], tables[1], select, masks[1]) + stacks,
        [(*rows, VMEM)] + saved_out + [(*rows, VMEM), (*halo, VMEM)], scratch, "layer_one")
    arrived = other_core(send)
    vectors = jnp.stack([merge_gain, merge_bias]).astype(F32)
    chunk = 768 if 768 % (dp * 16) == 0 else dp * 16
    total_rows = 6144 + -(-(2048 + 48) // chunk) * chunk
    merged, parts, merge_sums, grad_own, send = call(
        merge_kernel, at(VMEM, out1, arrived, own2, halo2, vectors, cot) + at(HBM, merge_weight, wm_other),
        [((2, merged_rows, 512), BF, VMEM), ((2, total_rows, 512), BF, HBM), ((8, 512), F32, VMEM), (*wide_rows, VMEM), (*halo, VMEM)],
        [((merged_rows, 2048), F32), ((merged_rows, 2048), BF), ((merged_rows, 2048), F32),
         ((2, 2048, 512), BF), ((2, 2048, 512), BF), 4], "merge")
    arrived = other_core(send)
    work = weight_shapes + saved_shapes + [
        rows, ((tokens, 2048), BF), rows, ((tokens, 1536), BF), wide_rows, ((heads * WP, WP), F32), ((48, 512), F32),
        ((6144, 512), BF), ((total_rows - 8192, 512), BF), 16]
    parts, grad_own, send, _ = call(
        backward1_kernel,
        at(VMEM, grad_own, arrived, own1, halo1, x1, small[1], select, back, merge_sums) + at(HBM, *saved1) + stacks + at(HBM, parts),
        [((2, total_rows, 512), BF, HBM), (*wide_rows, VMEM), (*halo, VMEM), (*wide_rows, VMEM)], work, "layer_one_back", {23: 0})
    arrived = other_core(send)
    parts, grad_x = call(
        backward0_kernel,
        at(VMEM, grad_own, arrived, send0, x0, small[0], select, back, merge_sums) + at(HBM, *saved0) + stacks + at(HBM, parts),
        [((2, total_rows, 512), BF, HBM), (*wide_rows, VMEM)], work, "layer_zero_back", {22: 0})

    grad_x = grad_x.reshape(pages * 2, WP, 512)[:, :AREA].reshape(pages, 2, 10, 10, 512)
    grad_x = grad_x.transpose(0, 2, 1, 3, 4).reshape(pages, 10, PAGE, 512)
    mine = lax.dynamic_slice_in_dim(grad_x, core * 256, 256, axis=3)
    yours = other_core(lax.dynamic_slice_in_dim(grad_x, (1 - core) * 256, 256, axis=3).astype(BF)).astype(F32)
    grad_pages = jnp.where(core == 0, jnp.concatenate([mine, yours], axis=1), jnp.concatenate([yours, mine], axis=1))

    merged = merged[:, : pages * 50].reshape(2, pages, 5, 10, 512)
    mine = lax.dynamic_index_in_dim(merged, core, 0, keepdims=False)
    yours = other_core(lax.dynamic_index_in_dim(merged, 1 - core, 0, keepdims=False))
    merged = jnp.where(core == 0, jnp.concatenate([mine, yours], axis=1), jnp.concatenate([yours, mine], axis=1))

    total = sum_rows(parts, dp, chunk)
    g_qkv, g_proj, g_fc1, g_fc2, g_merge, tail = call(
        widen_kernel, at(HBM, total),
        [((512, 1536), F32, HBM), ((512, 512), F32, HBM), ((512, 2048), F32, HBM), ((2048, 512), F32, HBM),
         ((2048, 512), F32, HBM), ((48, 512), F32, VMEM)],
        [((total_rows, 512), BF), ((4, 512, 512), F32), 17, 4], "widen")
    grad_table = tail[16:32, 3 : 3 + table][:, ::-1].T[None]
    return (
        merged, grad_pages, tail[0:1], tail[1:2], g_qkv[None], tail[2:3], tail[3:4], grad_table,
        g_proj[None], tail[4:5], tail[5:6], tail[6:7], g_fc1[None], tail[8:12].reshape(1, 2048),
        g_fc2[None], tail[7:8], tail[32:36].reshape(2048), tail[36:40].reshape(2048), g_merge,
    )


def solution(mesh):
    row, mat = P("pipe", None), P("pipe", None, None)
    wide = P("dp", None, None, "pipe")
    in_specs = (wide, row, row, mat, row, row, mat, mat, row, row, row, mat, row, mat, row, P(), P(), P(None, "pipe"), wide)
    out_specs = (wide, wide, row, row, mat, row, row, mat, mat, row, row, row, mat, row, mat, row, P(), P(), P(None, "pipe"))
    return jax.shard_map(shards, mesh=mesh, in_specs=in_specs, out_specs=out_specs, check_vma=False)
```

time: 1670 us -> 327 us (0.20)
  local copies, waits for them, and re-layouts: 620 us -> 27.6 us
  matrix products: 406 us -> 0 us
  Pallas kernels: 0 us -> 277 us
  waiting for transfers between devices: 263 us -> 4.61 us
  other arithmetic: 209 us -> 6.42 us
  blocking collectives: 127 us -> 0 us
  between operations: 18.5 us -> 1.41 us
    dot_general x98 -> x0, matrix products: 362 us -> none  [the longest x8 66.7 us: block_forward(): jnp.dot(activated, fc2_weight, preferred_element_type=jnp.float32)]
    pallas_call x0 -> x7, Pallas kernels: none -> 277 us  [the longest x1 152 us: sum_rows(): pl.pallas_call(functools.partial(comm_kernel, dp, count, chunk), out_shap...]
    psum x1 -> x0, waiting for transfers between devices: 263 us -> none  [shards(): lax.psum((grad_totals[0], grad_totals[1], grad_totals[2], grad_totals[3],...]
    reshape x77 -> x2, local copies, waits for them, and re-layouts: 165 us -> 0.74 us  [the longest x1 0.73 us: shards(): grad_x.reshape(pages * 2, WP, 512)[:, :AREA].reshape(pages, 2, 10, 10, 512)]
    convert_element_type x82 -> x1, local copies, waits for them, and re-layouts: 150 us -> 0.15 us  [shards(): lax.dynamic_slice_in_dim(grad_x, (1 - core) * 256, 256, axis=3).astype(BF)]
    psum x2 -> x0, blocking collectives: 127 us -> none  [the longest x1 82.2 us: shards(): lax.psum((grad_totals[0], grad_totals[1], grad_totals[2], grad_totals[3],...]
    reduce_sum x56 -> x0, other arithmetic: 86.5 us -> none  [the longest x24 34.1 us: norm_forward(): jnp.mean(centred * centred, axis=-1, keepdims=True) + norm_eps]
    transpose x44 -> x1, local copies, waits for them, and re-layouts: 68.5 us -> 0.42 us  [shards(): grad_x = grad_x.transpose(0, 2, 1, 3, 4).reshape(pages, 10, PAGE, 512)]
  transfers between devices with their start and end apart: 11 -> 15, of which waited for: 1 -> 7; matrix products, arithmetic and copies ran while one was open for 34% -> 7% of each run, Pallas kernels for 0% -> 12%
where the time goes in v1:
time: 327 us; the launch traced here: 322 us
  Pallas kernels  277 us (85%)
  local copies, waits for them, and re-layouts  27.6 us (8%)
  other arithmetic  6.42 us (2%)
  starting transfers between devices  4.65 us (1%)
  waiting for transfers between devices  4.61 us (1%)
    pallas_call x1, Pallas kernels, sum_rows(): pl.pallas_call(functools.partial(comm_kernel, dp, count, chunk), out_shap...  152 us
    pallas_call x6, Pallas kernels, call(): pl.pallas_call(kernel, out_shape=[jax.ShapeDtypeStruct(s, d) for s, d, _...  125 us
    unnamed x29, local copies, waits for them, and re-layouts  12.6 us
  transfers between devices with their start and end apart: 15, of which 7 were waited for; matrix products, arithmetic and copies ran while one was open for 7% of the time, Pallas kernels for 12%

profile of v1, /device:TPU:0, one launch (start us, length us, event | category | flops | bytes accessed | tf_op | source)
XLA Modules:
  0.0 321.6 jit_solution(7349417728663887802)
XLA Ops:
  0.7 0.5 collective-permute-start.5
  1.3 0.4 collective-permute-start.3
  1.7 0.8 slice.71
  2.5 1.5 reverse.1
  4.4 0.4 collective-permute-start.10
  5.0 0.7 reduce
  5.7 0.9 concatenate.24
  6.6 1.4 collective-permute-done.2
  8.1 1.0 constant_dynamic-slice_fusion.4
  9.1 0.7 stack.24
  9.8 0.7 stack.25
  10.5 0.4 collective-permute-start
  10.9 1.7 constant_dynamic-slice_fusion.3
  12.6 0.7 select_convert_fusion.2
  13.3 0.5 collective-permute-done
  13.8 0.4 collective-permute-start.4
  14.2 0.6 select_convert_fusion
  14.9 0.5 copy.62
  15.5 1.2 copy.75
  16.6 1.3 reshape.287
  18.0 0.9 pad.12.clone
  19.1 0.7 broadcast_in_dim.51.mask
  19.8 0.6 copy-done
  20.4 19.5 %layer_zero.1 = (bf16[672,1536]{1,0:T(8,128)(2,1)}, bf16[10752,112]{1,0:T(8,128)(2,1)}, bf16[672,512]{1,0:T(8,128)(2,1)}, f32[672,512]{1,0:T(8,128)}, bf16[672,2...) custom-call(bf16[672,512]{1,0:T(8,128)(2,1)} %bitcast.63, ...), custom_call_target="tpu_custom_call" | custom-call | tf_op jit(solution)/shard_map/layer_zero/pallas_call | solution.py:471
  39.9 0.4 collective-permute-start.7
  40.3 0.6 maximum_convert_fusion.vectors
  41.0 0.6 pad_maximum_fusion.1.mask
  41.8 0.7 copy-done.7
  42.5 20.4 %layer_one.1 = (bf16[672,512]{1,0:T(8,128)(2,1)}, bf16[672,1536]{1,0:T(8,128)(2,1)}, bf16[10752,112]{1,0:T(8,128)(2,1)}, bf16[672,512]{1,0:T(8,128)(2,1)}, f32[6...) custom-call(bf16[672,512]{1,0:T(8,128)(2,1)} %get-tuple-element.52.p, ...), custom_call_target="tpu_custom_call" | custom-call | tf_op jit(solution)/shard_map/layer_one/pallas_call | solution.py:471
  62.9 0.4 collective-permute-start.8
  63.7 0.8 fusion.2.cot
  64.5 0.3 collective-permute-done.8.arrived
  64.8 0.7 copy-done.8
  65.5 9.6 %merge.1 = (bf16[2,160,512]{2,1,0:T(8,128)(2,1)}, bf16[2,8448,512]{2,1,0:T(8,128)(2,1)}, f32[8,512]{1,0:T(8,128)}, f32[672,512]{1,0:T(8,128)}, bf16[304,512]{1,0:T(8,128)(2,1)}) custom-call(bf16[672,512]{1,0:T(8,128)(2,1)} %get-tuple-element.54.own, bf16[304,512]{1,0:T(8,128)(2,1)} %copy-done.8, bf16[640,672]{1,0:T(8,128)(2,1)} %constant.76.clone.own2, ...), custom_call_target="tpu_custom_call" | custom-call | tf_op jit(solution)/shard_map/merge/pallas_call | solution.py:471
  75.1 0.4 collective-permute-start.12
  75.6 1.0 slice.57
  76.6 0.2 copy.67
  76.8 0.2 collective-permute-done.12.arrived
  77.0 0.7 copy-done.6
  77.7 33.9 %layer_one_back.1 = (bf16[2,8448,512]{2,1,0:T(8,128)(2,1)}, f32[672,512]{1,0:T(8,128)}, bf16[304,512]{1,0:T(8,128)(2,1)}, f32[672,512]{1,0:T(8,128)}) custom-call(f32[672,512]{1,0:T(8,128)} %get-tuple-element.57.grad_own, bf16[304,512]{1,0:T(8,128)(2,1)} %copy-done.6, bf16[672,672]{1,0:T(8,128)(2,1)} %constant.74.clone.own1, ...), custom_call_target="tpu_custom_call", output_to_operand_aliasing={{0}: (23, {})} | custom-call | tf_op jit(solution)/shard_map/layer_one_back/pallas_call | solution.py:471
  111.7 0.4 collective-permute-start.13
  112.1 0.6 constant_dynamic-slice_fusion.2
  112.9 0.2 collective-permute-start.11
  113.2 1.2 collective-permute-done.11
  114.4 1.2 maximum_select_fusion.1
  115.6 0.7 copy-done.5
  116.3 32.0 %layer_zero_back.1 = (bf16[2,8448,512]{2,1,0:T(8,128)(2,1)}, f32[672,512]{1,0:T(8,128)}) custom-call(f32[672,512]{1,0:T(8,128)} %get-tuple-element.68.grad_own, bf16[304,512]{1,0:T(8,128)(2,1)} %copy-done.5, bf16[304,672]{1,0:T(8,128)(2,1)} %constant.73.clone.send0, bf16[672,512]{1,0:T(8,128)(2,1)} %bitcast.64, ...), custom_call_target="tpu_custom_call", output_to_operand_aliasing={{0}: (22, {})} | custom-call | tf_op jit(solution)/shard_map/layer_zero_back/pallas_call | solution.py:471
  148.3 152.1 %sum_rows.1.total = bf16[8448,512]{1,0:T(8,128)(2,1)} custom-call(bf16[2,8448,512]{2,1,0:T(8,128)(2,1)} %get-tuple-element.78.parts), custom_call_target="tpu_custom_call" | custom-call | tf_op jit(solution)/shard_map/sum_rows/pallas_call | solution.py:646
  300.5 9.3 %widen.1 = (f32[512,1536]{1,0:T(8,128)}, f32[512,512]{1,0:T(8,128)}, f32[512,2048]{1,0:T(8,128)}, f32[2048,512]{1,0:T(8,128)}, f32[2048,512]{1,0:T(8,128)}, /*index=5*/f32[48,512]{1,0:T(8,128)}) custom-call(bf16[8448,512]{1,0:T(8,128)(2,1)} %sum_rows.1.total), custom_call_target="tpu_custom_call" | custom-call | tf_op jit(solution)/shard_map/widen/pallas_call | solution.py:471
  309.8 0.8 slice.63
  310.6 0.8 slice_bitcast_fusion
  311.4 1.6 fusion.4
  313.1 0.2 reverse.2
  313.3 0.6 copy.77
  313.9 0.6 copy.78
  314.5 0.6 copy.79
  315.2 0.7 copy.73
  316.0 0.7 reshape.282
  316.7 0.4 copy.71
  317.5 0.7 slice_bitcast_fusion.3
  318.2 0.9 collective-permute-done.14
  319.1 0.2 convert_element_type.47
  319.3 0.5 maximum_select_fusion
  319.8 1.3 copy.72
  (48 shorter events, 2.3 us)
Async XLA Ops:
  0.7 14.2 %copy-start.3 = (bf16[3,20,20,256]{3,2,1,0:T(8,128)(2,1)S(1)}, bf16[3,20,20,256]{3,2,1,0:T(8,128)(2,1)}, u32[]{:S(2)}) copy-start(bf16[3,20,20,256]{3,2,1,0:T(8,128)(2,1)} %param.26) | copy-start | bytes 1843204
  0.7 18.4 %collective-permute-start.5 = (bf16[512,2048]{1,0:T(8,128)(2,1)}, bf16[512,2048]{1,0:T(8,128)(2,1)S(1)}, u32[]{:S(2)}, u32[]{:S(2)}) collective-permute-start(bf16[512,2048]{1,0:T(8,128)(2,1)} %bitcast.43), channel_id=1, source_target_pairs={{0,16},{16,0},{1,17},{17,1},{2,18},{18,2},{3,19},{19,3},{4,20},{20... | collective-permute-start | bytes 6291464 | tf_op jit(solution)/shard_map/ppermute | solution.py:484
  1.2 17.9 %collective-permute-start.6 = (bf16[2048,512]{1,0:T(8,128)(2,1)}, bf16[2048,512]{1,0:T(8,128)(2,1)}, u32[]{:S(2)}, u32[]{:S(2)}) collective-permute-start(bf16[2048,512]{1,0:T(8,128)(2,1)} %bitcast.48), channel_id=1, source_target_pairs={{0,16},{16,0},{1,17},{17,1},{2,18},{18,2},{3,19},{19,3},{4,20},{20... | collective-permute-start | bytes 6291464 | tf_op jit(solution)/shard_map/ppermute | solution.py:484
  1.3 17.8 %collective-permute-start.3 = (bf16[512,1536]{1,0:T(8,128)(2,1)}, bf16[512,1536]{1,0:T(8,128)(2,1)}, u32[]{:S(2)}, u32[]{:S(2)}) collective-permute-start(bf16[512,1536]{1,0:T(8,128)(2,1)} %bitcast.53), channel_id=1, source_target_pairs={{0,16},{16,0},{1,17},{17,1},{2,18},{18,2},{3,19},{19,3},{4,20},{20... | collective-permute-start | bytes 4718600 | tf_op jit(solution)/shard_map/ppermute | solution.py:484
  4.3 3.6 %collective-permute-start.2 = (bf16[16,384]{1,0:T(8,128)(2,1)S(1)}, bf16[16,384]{1,0:T(8,128)(2,1)S(1)}, u32[]{:S(2)}, u32[]{:S(2)}) collective-permute-start(bf16[16,384]{1,0:T(8,128)(2,1)S(1)} %pad_maximum_fusion.2), channel_id=1, source_target_pairs={{0,16},{16,0},{1,17},{17,1},{2,18},{18,2},{3,19},{19,3},{4,20},{20... | collective-permute-start | bytes 36872 | tf_op jit(solution)/shard_map/ppermute | solution.py:484
  4.4 60.1 %collective-permute-start.10 = (bf16[2048,512]{1,0:T(8,128)(2,1)}, bf16[2048,512]{1,0:T(8,128)(2,1)}, u32[]{:S(2)}, u32[]{:S(2)}) collective-permute-start(bf16[2048,512]{1,0:T(8,128)(2,1)} %wm_own.1), channel_id=1, source_target_pairs={{0,16},{16,0},{1,17},{17,1},{2,18},{18,2},{3,19},{19,3},{4,20},{20... | collective-permute-start | bytes 6291464 | tf_op jit(solution)/shard_map/ppermute | solution.py:484
  7.9 2.5 collective-permute-start.1
  10.5 3.3 %collective-permute-start = (bf16[3,10,20,256]{3,2,1,0:T(8,128)(2,1)S(1)}, bf16[3,10,20,256]{3,2,1,0:T(8,128)(2,1)S(1)}, u32[]{:S(2)}, u32[]{:S(2)}) collective-permute-start(bf16[3,10,20,256]{3,2,1,0:T(8,128)(2,1)S(1)} %constant_dynamic-slice_fusion.4), channel_id=1, source_target_pairs={{0,16},{16,0},{1,17},{17,1},{2,18},{18,2},{3,19},{19,3},{4,20},{20... | collective-permute-start | bytes 921608 | tf_op jit(solution)/shard_map/ppermute | solution.py:484
  13.8 5.1 %collective-permute-start.4 = (bf16[512,512]{1,0:T(8,128)(2,1)}, bf16[512,512]{1,0:T(8,128)(2,1)S(1)}, u32[]{:S(2)}, u32[]{:S(2)}) collective-permute-start(bf16[512,512]{1,0:T(8,128)(2,1)} %bitcast.58), channel_id=1, source_target_pairs={{0,16},{16,0},{1,17},{17,1},{2,18},{18,2},{3,19},{19,3},{4,20},{20... | collective-permute-start | bytes 1572872 | tf_op jit(solution)/shard_map/ppermute | solution.py:484
  18.9 0.9 copy-start.1
  18.9 44.4 %collective-permute-start.9 = (bf16[3,5,10,512]{3,0,2,1:T(4,128)(2,1)}, bf16[3,5,10,512]{3,0,2,1:T(4,128)(2,1)S(1)}, u32[]{:S(2)}, u32[]{:S(2)}) collective-permute-start(bf16[3,5,10,512]{3,0,2,1:T(4,128)(2,1)} %constant_dynamic-slice_fusion.3), channel_id=1, source_target_pairs={{0,16},{16,0},{1,17},{17,1},{2,18},{18,2},{3,19},{19,3},{4,20},{20... | collective-permute-start | bytes 460808 | tf_op jit(solution)/shard_map/ppermute | solution.py:484
  19.1 1.4 copy-start
  39.9 1.9 collective-permute-start.7
  41.8 0.7 copy-start.7
  42.5 20.8 %copy-start.4 = (bf16[3,10,10,512]{3,0,2,1:T(4,128)(2,1)S(1)}, bf16[3,10,10,512]{3,0,2,1:T(4,128)(2,1)}, u32[]{:S(2)}) copy-start(bf16[3,10,10,512]{3,0,2,1:T(4,128)(2,1)} %param.44) | copy-start | bytes 921604
  62.9 1.9 collective-permute-start.8
  64.8 0.7 copy-start.8
  75.1 1.9 collective-permute-start.12
  77.0 0.7 copy-start.6
  111.7 3.9 %collective-permute-start.13 = (bf16[304,512]{1,0:T(8,128)(2,1)}, bf16[304,512]{1,0:T(8,128)(2,1)S(1)}, u32[]{:S(2)}, u32[]{:S(2)}) collective-permute-start(bf16[304,512]{1,0:T(8,128)(2,1)} %get-tuple-element.69), channel_id=1, source_target_pairs={{0,16},{16,0},{1,17},{17,1},{2,18},{18,2},{3,19},{19,3},{4,20},{20... | collective-permute-start | bytes 933896 | tf_op jit(solution)/shard_map/ppermute | solution.py:484
  112.9 1.5 collective-permute-start.11
  115.6 0.7 copy-start.5
  300.5 14.6 %copy-start.2 = (f32[672,512]{1,0:T(8,128)S(1)}, f32[672,512]{1,0:T(8,128)}, u32[]{:S(2)}) copy-start(f32[672,512]{1,0:T(8,128)} %get-tuple-element.77) | copy-start | bytes 4128772
  317.3 1.8 collective-permute-start.14

commit v2 on v1

v2 whole, which is shorter than its diff:
```python
from functools import partial

import jax
import jax.numpy as jnp
import numpy as np
from jax import lax
from jax.experimental import pallas as pl
from jax.experimental.pallas import tpu as pltpu
from jax.sharding import PartitionSpec as P

BF = jnp.bfloat16
F32 = jnp.float32
WINDOW = 10
AREA = 100
PAGE = 20
WP = 112
EPS = 1e-05
NEG = -1e30
MESH = pl.DeviceIdType.MESH
CHIPS = 16
STEPS = 8
UNIT = 256
CHUNK = 768
ROWS = 8448
SLOT = CHUNK + CHUNK // 8
RING = 4
VMEM_LIMIT = 62 * 1024 * 1024
EMITS = [(r, r + 512) for r in range(0, 8192, 512)] + [(8192, 8448)]
KINDS = (0, 2, 0, 1, 1, 3, 1, 0, 0, 1, 2)
SCHEDULE = (
    ((1, 3, 6, 8, 9, 10, 12, 15, 17), (1, 3, 6, 8, 9, 10, 12, 15, 17), (14, 16, 18, 21, 23, 30, 36, 46, 56), (14, 16, 18, 22, 28, 32, 38, 46, 56), (15, 17, 19, 25, 31, 35, 44, 53, 59), (16, 21, 27, 34, 37, 41, 48, 55, 61), (16, 21, 27, 34, 37, 42, 50, 57, 63), (16, 21, 27, 34, 39, 45, 51, 57, 63), (20, 26, 33, 38, 43, 49, 54, 60, 64), (20, 26, 33, 40, 47, 52, 58, 62, 65), (24, 29, 36, 40, 47, 52, 58, 62, 66)),
    ((1, 4, 6, 7, 8, 9, 10, 12, 16), (1, 4, 6, 7, 8, 9, 10, 12, 16), (2, 5, 7, 9, 10, 13, 16, 18, 23), (2, 5, 7, 9, 10, 13, 16, 18, 23), (3, 6, 8, 9, 10, 13, 17, 18, 25), (4, 6, 8, 9, 10, 13, 17, 20, 28), (4, 7, 9, 10, 14, 16, 18, 24, 31), (4, 7, 9, 11, 14, 16, 19, 29, 31), (9, 11, 14, 17, 18, 21, 30, 34, 38), (9, 11, 14, 18, 22, 27, 33, 36, 39), (10, 13, 17, 18, 26, 32, 35, 37, 40)),
)
FALLBACK = (((19,),) * 11, ((19,),) * 11)


def mm(a, b):
    return lax.dot_general(a, b, (((1,), (0,)), ((), ())), preferred_element_type=F32)


def mm_nt(a, b):
    return lax.dot_general(a, b, (((1,), (1,)), ((), ())), preferred_element_type=F32)


def mm_tn(a, b):
    return lax.dot_general(a, b, (((0,), (0,)), ((), ())), preferred_element_type=F32)


def unit_norm(values):
    centred = values - jnp.mean(values, axis=-1, keepdims=True)
    inv_std = lax.rsqrt(jnp.mean(centred * centred, axis=-1, keepdims=True) + EPS)
    return centred * inv_std, inv_std


def unit_norm_back(grad_normed, unit_rows, inv_std, gain):
    grad_unit = grad_normed * gain
    return inv_std * (
        grad_unit
        - jnp.mean(grad_unit, axis=-1, keepdims=True)
        - unit_rows * jnp.mean(grad_unit * unit_rows, axis=-1, keepdims=True)
    )


def place_tables(pages):
    merged = -(-pages * 50 // 16) * 16
    group = -(-pages // 4) * 4
    cots = AREA * group
    take = np.zeros((2, 2 * WP, 400), np.float32)
    pick = np.zeros((2, merged, cots), np.float32)
    send0 = np.zeros((WP, 2 * WP), np.float32)
    own1 = np.zeros((2 * WP, 2 * WP), np.float32)
    halo1 = np.zeros((2 * WP, WP), np.float32)
    own2 = np.zeros((4 * merged, pages * 2 * WP), np.float32)
    halo2 = np.zeros((4 * merged, pages * WP), np.float32)

    def row0(r, col):
        return col // WINDOW * WP + r * WINDOW + col % WINDOW

    def row1(r, col):
        return row0(r, (col - 5) % PAGE)

    for col in range(PAGE):
        for r in range(10):
            for core in range(2):
                take[core, row0(r, col), (core * 10 + r) * PAGE + col] = 1
        for r in range(5):
            send0[r * PAGE + col, row0(r, col)] = 1
            own1[row1(r, col), row0(r + 5, col)] = 1
            halo1[row1(r + 5, col), r * PAGE + col] = 1
    for p in range(pages):
        for m in range(5):
            for n in range(10):
                for core in range(2):
                    pick[core, p * 50 + m * 10 + n, ((core * 5 + m) * 10 + n) * group + p] = 1
                for k in range(4):
                    row = k * merged + p * 50 + m * 10 + n
                    r, col = 2 * m + k % 2, 2 * n + k // 2
                    if r >= 5:
                        own2[row, p * 2 * WP + row1(r - 5, col)] = 1
                    else:
                        halo2[row, p * WP + r * PAGE + col] = 1
    return {name: jnp.asarray(t, BF) for name, t in dict(
        take=take, back=take.transpose(0, 2, 1), pick=pick, send0=send0, own1=own1, halo1=halo1, own2=own2, halo2=halo2).items()}


def window_masks():
    place = np.arange(WP)
    pad = np.where(place < AREA, 0.0, NEG)
    masks = np.zeros((3, 2, WP, WP), np.float32)
    for kind in range(3):
        for side in range(2):
            late = (place // WINDOW >= 5) * 2 * (kind == 2) + (place % WINDOW >= 5) * (side == 1) * (kind > 0)
            masks[kind, side] = np.where(late[:, None] != late[None, :], -100.0, 0.0) + pad[None, :]
    return jnp.asarray(masks)


def by_page(pages, matrix, rows):
    count = matrix.shape[1]
    return jnp.concatenate([mm(matrix[...], rows[p * count : (p + 1) * count]) for p in range(pages)], axis=0)


def by_page_back(pages, matrix, rows):
    count = matrix.shape[0]
    return jnp.concatenate([mm_tn(matrix[...], rows[p * count : (p + 1) * count]) for p in range(pages)], axis=0)


def code_matrices():
    select = np.zeros((WP, 384), np.float32)
    back = np.zeros((184, WP), np.float32)
    for i in range(AREA):
        code = (i // WINDOW) * 19 + i % WINDOW
        select[i, code] = 1
        back[183 - code, i] = 1
    return jnp.asarray(select, BF), jnp.asarray(back, BF)


def expand_table(table, select, pos):
    entries = table[...].astype(F32)
    for h in range(table.shape[0]):
        spread = pltpu.roll(jnp.broadcast_to(entries[h : h + 1, :], (184, 384)), 208, 1, stride=1, stride_axis=0)
        rows = mm(select[:, 0:184], spread.astype(BF)).astype(BF)
        pos[h * WP : (h + 1) * WP, :] = mm_nt(rows, select[...]).astype(BF)


def reduce_table(score, select, back, out):
    for h in range(out.shape[0]):
        block = score[h * WP : (h + 1) * WP, :].astype(BF)
        codes = mm(back[...], mm(block, select[:, 0:256]).astype(BF))
        codes = jnp.concatenate([codes, jnp.zeros((184, 128), F32)], axis=1)
        turned = pltpu.roll(codes, 0, 1, stride=1, stride_axis=0)
        out[h : h + 1, 0:384] = jnp.sum(turned, axis=0, keepdims=True)


def head_masks(kind):
    lane = lax.broadcasted_iota(jnp.int32, (1, 128), 1) // 32
    return [jnp.where(lane == h, 1.0, 0.0).astype(kind) for h in range(4)]


def stack_heads(block, masks):
    return jnp.concatenate([block * mask for mask in masks], axis=0)


def pick_heads(stacked, masks):
    total = stacked[0:WP] * masks[0]
    for h in range(1, 4):
        total = total + stacked[h * WP : (h + 1) * WP] * masks[h]
    return total


def block_forward(x_ref, small, weights, ready, pos, mask, bufs, n_ref, keep, free):
    qkv, attn, attended, hidden, act, dgelu = bufs
    wqkv, wproj, wfc1, _ = weights
    tokens = x_ref.shape[0]
    unit_one, _ = unit_norm(x_ref[...].astype(F32))
    n_ref[...] = (unit_one * small[0:1] + small[1:2]).astype(BF)
    zero = jnp.zeros((1, 512), F32)
    bias = [small[2:3], zero, small[3:4]]
    ready(0)
    free(0)
    for j in range(6):
        shift = bias[j // 2][:, (j % 2) * 256 : (j % 2) * 256 + 256]
        qkv[:, j * 256 : j * 256 + 256] = (mm(n_ref[...], wqkv[:, j * 256 : j * 256 + 256]) + shift).astype(BF)
    keep(0)
    free(1)
    free(2)
    low_masks, masks = head_masks(BF), head_masks(F32)

    def window(w, carry):
        rows = aligned(w * WP, WP)
        side = mask[w % 2]
        for blk in range(4):
            q, k, v = [qkv[rows, i * 512 + blk * 128 : i * 512 + blk * 128 + 128] for i in range(3)]
            s = mm_nt(stack_heads(q, low_masks), k) * 32**-0.5
            s = s + pos[blk * 4 * WP : (blk + 1) * 4 * WP, :].astype(F32)
            s = (s.reshape(4, WP, WP) + side[None]).reshape(4 * WP, WP)
            e = jnp.exp(s - jnp.max(s, axis=-1, keepdims=True))
            a = (e * (1.0 / jnp.sum(e, axis=-1, keepdims=True))).astype(BF)
            attn[aligned((w * 4 + blk) * 4 * WP, 4 * WP), :] = a
            attended[rows, blk * 128 : blk * 128 + 128] = pick_heads(mm(a, v), masks).astype(BF)
        return carry

    lax.fori_loop(0, tokens // WP, window, 0, unroll=3)
    keep(1)
    keep(2)
    ready(1)
    free(3)
    for j in range(2):
        cols = slice(j * 256, j * 256 + 256)
        hidden[:, cols] = x_ref[:, cols].astype(F32) + (mm(attended[...], wproj[:, cols]) + small[4:5, cols])
    keep(3)
    unit_two, _ = unit_norm(hidden[...])
    n_ref[...] = (unit_two * small[5:6] + small[6:7]).astype(BF)
    ready(2)
    free(4)
    free(5)
    for j in range(8):
        cols = slice(j * 256, j * 256 + 256)
        u = mm(n_ref[...], wfc1[:, cols]) + small[8 + j // 2 : 9 + j // 2, (j % 2) * 256 : (j % 2) * 256 + 256]
        cdf = 0.5 + 0.5 * lax.erf(u * (0.5**0.5))
        act[:, cols] = (u * cdf).astype(BF)
        dgelu[:, cols] = (cdf + u * (jnp.exp(u * u * -0.5) * ((2 * np.pi) ** -0.5))).astype(BF)
    keep(4)
    keep(5)
    ready(3)


def layer_out(bufs, weights, small, out):
    hidden, act = bufs[3], bufs[4]
    for j in range(2):
        cols = slice(j * 256, j * 256 + 256)
        out[:, cols] = (hidden[:, cols] + (mm(act[...], weights[3][:, cols]) + small[7:8, cols])).astype(BF)


def forward_kernel(xh, cot, gain_one, bias_one, query_bias, value_bias, proj_bias, gain_two, bias_two, fc2_bias, fc1_bias,
                   merge_gain, merge_bias, table, turned, masks, take, pick, send0, own1, halo1, own2, halo2, select, *refs):
    own, saved, other = refs[0:5], (refs[5:12], refs[12:19]), refs[19:23]
    merged, normed, grad_cots, merge_sums, small, grad = refs[23:29]
    weights, wm, bufs = (refs[29:33], refs[33:37]), refs[37], refs[38:44]
    x_ref, n_ref, pos, rows_in, pack_in, cots, out, halo_out, halo_in = refs[44:53]
    rows_ref, ghead, msel, mrecv = refs[53:57]
    load_sem, keep_sem, other_sem, send_sem, recv_sem = refs[57:62]
    core, me = lax.axis_index("pipe"), lax.axis_index("dp")
    partner = 1 - core
    pages = x_ref.shape[0] // (2 * WP)

    def remote(i, source, target):
        return pltpu.make_async_remote_copy(
            src_ref=source, dst_ref=target, send_sem=send_sem.at[i], recv_sem=recv_sem.at[i],
            device_id=(partner, me), device_id_type=MESH)

    shared = [(xh, rows_in), (pack_in.at[core], pack_in), (cot, cots), (own[4], wm)]
    local = [pltpu.make_async_copy(source, target.at[core], load_sem.at[4 + i]) for i, (source, target) in enumerate(shared)]
    sends = [remote(4 + i, source, target.at[core]) for i, (source, target) in enumerate(shared)]
    gets = [remote(4 + i, source, target.at[partner]) for i, (source, target) in enumerate(shared)]

    def loading(layer, i):
        return pltpu.make_async_copy(own[i], weights[layer][i], load_sem.at[i])

    def pushing(layer, i):
        return remote(i, own[i], weights[layer][i])

    def each_core(action):
        for layer in range(2):
            @pl.when(core == layer)
            def _():
                action(layer)

    local[0].start()

    def load(layer):
        for i in range(4):
            loading(layer, i).start()

    each_core(load)
    local[2].start()
    local[3].start()
    singles = [gain_one, bias_one, query_bias, value_bias, proj_bias, gain_two, bias_two, fc2_bias]
    rows = [row[...].astype(F32) for row in singles] + [fc1_bias[:, k * 512 : k * 512 + 512].astype(F32) for k in range(4)]
    pack_in[core, 0:16, :] = jnp.concatenate(rows + [jnp.zeros((4, 512), F32)], axis=0).astype(BF)
    entries = mm(table[...], turned[...]).astype(BF)
    pack_in[core, 16:32, :] = jnp.concatenate([entries, jnp.zeros((16, 128), BF)], axis=1)
    barrier = pltpu.get_barrier_semaphore()
    pl.semaphore_signal(barrier, inc=1, device_id=(partner, me), device_id_type=MESH)
    pl.semaphore_wait(barrier, 1)
    sends[1].start()
    sends[0].start()

    def push(layer):
        for i in range(4):
            pushing(layer, i).start()

    each_core(push)
    sends[2].start()
    sends[3].start()

    def ready(layer):
        def wait(i):
            @pl.when(core == layer)
            def _():
                loading(layer, i).wait()

            @pl.when(core != layer)
            def _():
                pushing(layer, i).wait_recv()
                pltpu.make_async_copy(weights[layer][i], other[i], other_sem.at[i]).start()

        return wait

    def kept(layer, i):
        source = bufs[i] if i < 6 else x_ref
        return pltpu.make_async_copy(source, saved[layer][i], keep_sem.at[layer, i])

    gets[1].wait_recv()
    small[...] = pack_in[:, 0:16, :].astype(F32)
    expand_table(pack_in.at[0, 16:32, 0:384], select, pos)
    local[0].wait()
    gets[0].wait_recv()
    for half in range(2):
        for p in range(pages):
            x_ref[p * 2 * WP : (p + 1) * 2 * WP, half * 256 : half * 256 + 256] = mm(
                take[core], rows_in[half, p * 400 : (p + 1) * 400, :]).astype(BF)
    kept(0, 6).start()
    block_forward(x_ref, small[0], weights[0], ready(0), pos, masks.at[0], bufs, n_ref,
                  lambda i: kept(0, i).start(), lambda i: None)
    layer_out(bufs, weights[0], small[0], out)
    halo_out[0] = by_page(pages, send0, out).astype(BF)
    halo = [remote(8 + i, halo_out.at[i], halo_in.at[i]) for i in range(3)]
    halo[0].start()
    expand_table(pack_in.at[1, 16:32, 0:384], select, pos)
    kept(0, 6).wait()
    x_ref[...] = by_page(pages, own1, out).astype(BF)
    halo[0].wait_recv()
    x_ref[...] = x_ref[...] + by_page(pages, halo1, halo_in[0]).astype(BF)
    kept(1, 6).start()
    block_forward(x_ref, small[1], weights[1], ready(1), pos, masks.at[1 + core], bufs, n_ref,
                  lambda i: kept(1, i).start(), lambda i: kept(0, i).wait())
    layer_out(bufs, weights[1], small[1], out)
    halo_out[1] = by_page_back(pages, halo1, out).astype(BF)
    halo[1].start()

    count = rows_ref.shape[0]
    local[2].wait()
    gets[2].wait_recv()
    for half in range(2):
        grad_cots[half] = mm(pick[core], cots[half]).astype(BF)
    for k in range(4):
        rows_ref[:, k * 512 : k * 512 + 512] = mm(own2[k * count : (k + 1) * count, :], out[...])
    halo[1].wait_recv()
    for k in range(4):
        cols = slice(k * 512, k * 512 + 512)
        rows_ref[:, cols] = rows_ref[:, cols] + mm(halo2[k * count : (k + 1) * count, :], halo_in[1])
    unit, inv_std = unit_norm(rows_ref[...])
    scale, shift = [jnp.concatenate([v[i : i + 1].astype(F32) for i in range(16)], axis=1) for v in (merge_gain[...], merge_bias[...])]
    normed[...] = (unit * scale + shift).astype(BF)
    local[3].wait()
    gets[3].wait_recv()
    for half in range(2):
        for k in range(4):
            cols = slice(k * 512, k * 512 + 512)
            term = mm_nt(grad_cots[half], wm[half, cols, :]).astype(BF).astype(F32)
            ghead[:, cols] = term if half == 0 else ghead[:, cols] + term
    grad_head = ghead[...]
    over_rows = [jnp.sum(grad_head * unit, axis=0, keepdims=True), jnp.sum(grad_head, axis=0, keepdims=True)]
    for i in range(2):
        for k in range(4):
            merge_sums[i * 4 + k : i * 4 + k + 1] = over_rows[i][:, k * 512 : k * 512 + 512]
    grad_rows = unit_norm_back(grad_head, unit, inv_std, scale).astype(BF)
    stacked = jnp.concatenate([grad_rows[:, k * 512 : k * 512 + 512] for k in range(4)], axis=0)
    halo_out[2] = mm_tn(halo2[...], stacked).astype(BF)
    halo[2].start()
    grad[...] = mm_tn(own2[...], stacked)
    for half in range(2):
        msel[half] = mm(normed[...], wm[half]).astype(BF)
    rows_copy = remote(11, msel.at[partner], mrecv)
    rows_copy.start()
    halo[2].wait_recv()
    grad[...] = grad[...] + by_page(pages, halo1, halo_in[2])
    rows_copy.wait_recv()
    merged[...] = (mm_tn(pick[core], msel[core]) + mm_tn(pick[partner], mrecv[...])).astype(BF)

    for copy in sends + halo + [rows_copy]:
        copy.wait_send()
    for i in range(7):
        kept(1, i).wait()

    def settle(layer):
        for i in range(4):
            pushing(layer, i).wait_send()
            pltpu.make_async_copy(weights[1 - layer][i], other[i], other_sem.at[i]).wait()

    each_core(settle)


class Chips:
    def __init__(self):
        me = lax.axis_index("dp")
        x, y, low, high = [lax.rem(me // stride, 2) for stride in (1, 2, 4, 8)]
        self.along_x = (me + 1 - 2 * x, x)
        self.along_y = (me + 2 - 4 * y, y)
        self.inner = lax.rem(low + high, 2)
        self.near_z = (me + 4 - 8 * low, self.inner)
        self.far_z = (me + 12 - 8 * low - 16 * high, high)


def aligned(start, count, step=16):
    return pl.ds(pl.multiple_of(start, step), count)


class Exchange:
    def __init__(self, dp, acc, paired, slots, total, sems):
        self.core, self.me = lax.axis_index("pipe"), lax.axis_index("dp")
        self.partner = 1 - self.core
        self.acc, self.paired, self.slots = acc, paired, slots
        self.total = total
        self.pair_send, self.pair_recv, self.store_sem, self.send_sem, self.recv_sem = sems
        self.chips = Chips() if dp == CHIPS else None
        self.steps = STEPS if self.chips else 0
        self.table = SCHEDULE if self.chips else FALLBACK

    def greet(self):
        barrier = pltpu.get_barrier_semaphore()
        chips = self.chips
        peers = [chip for chip, _ in (chips.along_x, chips.along_y, chips.near_z, chips.far_z)] if chips else []
        pl.semaphore_signal(barrier, inc=1, device_id=(self.partner, self.me), device_id_type=MESH)
        for chip in peers:
            pl.semaphore_signal(barrier, inc=1, device_id=(self.core, chip), device_id_type=MESH)
        pl.semaphore_wait(barrier, 1 + len(peers))

    def to_partner(self, unit, source):
        return pltpu.make_async_remote_copy(
            src_ref=source, dst_ref=self.paired.at[aligned(unit * UNIT, UNIT)],
            send_sem=self.pair_send.at[unit], recv_sem=self.pair_recv.at[unit],
            device_id=(self.partner, self.me), device_id_type=MESH)

    def ring_units(self, number):
        start, stop = EMITS[number]
        first = ROWS + number % RING * 512
        return [(start // UNIT + i, self.acc.at[first + i * UNIT : first + (i + 1) * UNIT])
                for i in range((stop - start) // UNIT)]

    def emit(self, number, owner, value):
        start, stop = EMITS[number]
        if number >= RING:
            @pl.when(jnp.logical_not(owner))
            def _():
                for unit, source in self.ring_units(number - RING):
                    self.to_partner(unit, source).wait_send()

        place = jnp.where(owner, start, ROWS + number % RING * 512)
        self.acc[aligned(place, stop - start), :] = value

        @pl.when(jnp.logical_not(owner))
        def _():
            for unit, source in self.ring_units(number):
                self.to_partner(unit, source).start()

    def kind_of(self, q):
        kind = jnp.int32(0)
        for i, k in enumerate(KINDS):
            kind = jnp.where(q == i, k, kind) if k else kind
        return kind

    def step_of(self, q, kind, step, z_last):
        chips = self.chips
        swapped = lax.rem(kind, 2)
        first = [jnp.where(swapped == 0, u, v) for u, v in zip(chips.along_x, chips.along_y)]
        second = [jnp.where(swapped == 0, u, v) for u, v in zip(chips.along_y, chips.along_x)]
        order = [first, second, chips.near_z, chips.far_z] if z_last else [chips.near_z, chips.far_z, first, second]
        lengths = [CHUNK // 2, CHUNK // 4, CHUNK // 4 if z_last else CHUNK // 8, CHUNK // 8 if z_last else CHUNK // 16]
        base = q * CHUNK
        for i in range(step):
            if not (z_last and i == 2):
                base = base + order[i][1] * lengths[i]
        chip, keep = order[step]
        length = lengths[step]
        slot = q * SLOT + sum(lengths[:step])
        if z_last and step == 2:
            return chip, base, base, length, slot, chips.inner == 0, chips.inner == 1
        when = chips.inner == 1 if z_last and step == 3 else None
        return chip, base + (1 - keep) * length, base + keep * length, length, slot, when, when

    def move(self, q, kind, e, z_last):
        half = STEPS // 2
        chip, give, keep, length, slot, sends, gets = self.step_of(q, kind, min(e, STEPS - 1 - e), z_last)
        target = aligned(slot, length)
        if e < half:
            ends = dict(src_ref=self.acc.at[aligned(give, length)], dst_ref=self.slots.at[target])
        else:
            sends, gets = gets, sends
            ends = dict(src_ref=self.paired.at[aligned(keep, length)], dst_ref=self.paired.at[aligned(keep, length)])
        copy = pltpu.make_async_remote_copy(
            send_sem=self.send_sem.at[q, e], recv_sem=self.recv_sem.at[q, e],
            device_id=(self.core, chip), device_id_type=MESH, **ends)
        return copy, sends, gets, aligned(keep, length), target

    def begin_step(self, q, kind, e, z_last):
        copy, sends, _, _, _ = self.move(q, kind, e, z_last)
        if sends is None:
            copy.start()
        else:
            pl.when(sends)(copy.start)

    def end_step(self, q, kind, e, z_last):
        copy, sends, gets, kept, target = self.move(q, kind, e, z_last)

        def got():
            copy.wait_recv()
            if e < STEPS // 2:
                into = self.acc if e < STEPS // 2 - 1 else self.paired
                into[kept, :] = (self.acc[kept, :].astype(F32) + self.slots[target, :].astype(F32)).astype(BF)

        if sends is None:
            got()
            copy.wait_send()
        else:
            pl.when(gets)(got)
            pl.when(sends)(copy.wait_send)

    def store(self, q):
        rows = aligned(q * CHUNK, CHUNK)
        return pltpu.make_async_copy(self.paired.at[rows], self.total.at[rows], self.store_sem.at[q])

    def event(self, q, e):
        if e == 0:
            into = self.acc if self.steps else self.paired

            def add(i, carry):
                unit = q * (CHUNK // UNIT) + i
                rows = aligned(unit * UNIT, UNIT)
                self.to_partner(unit, self.acc.at[rows]).wait_recv()
                into[rows, :] = (self.acc[rows, :].astype(F32) + self.paired[rows, :].astype(F32)).astype(BF)
                return carry

            lax.fori_loop(0, CHUNK // UNIT, add, 0)
        if self.steps:
            kind = self.kind_of(q)
            for z_last in (True, False):
                @pl.when(kind < 2 if z_last else kind >= 2)
                def _():
                    if e > 0:
                        self.end_step(q, kind, e - 1, z_last)
                    if e < STEPS:
                        self.begin_step(q, kind, e, z_last)

        if e == self.steps:
            self.store(q).start()

    def tick(self, t, done):
        def counts(table):
            def among(ticks, low, high):
                if low == high:
                    return jnp.int32(low)
                middle = (low + high) // 2
                return jnp.where(t >= ticks[middle], among(ticks, middle + 1, high), among(ticks, low, middle))

            return [among([chunk[e] for chunk in table], 0, len(table)) for e in range(self.steps + 1)]

        upto = lax.cond(self.core == 0, lambda: counts(self.table[0]), lambda: counts(self.table[1]))
        for e in reversed(range(self.steps + 1)):
            def one(q, carry):
                self.event(q, e)
                return carry

            lax.fori_loop(done[e], upto[e], one, 0)
        return upto

    def end(self):
        def stored(q, carry):
            self.store(q).wait()
            return carry

        lax.fori_loop(0, ROWS // CHUNK, stored, 0)

        for number in range(len(EMITS) - RING, len(EMITS)):
            for unit, source in self.ring_units(number):
                self.to_partner(unit, source).wait_send()


def backward_kernel(dp, grad_own, own1, halo1, send0, place_back, small, select, back, merge_sums, *refs):
    saved = (refs[0:7], refs[7:14])
    own, other, normed_hbm, cots_hbm = refs[14:18], refs[18:22], refs[22], refs[23]
    total, grad_x = refs[24:26]
    bufs, weights, refs = refs[26:33], refs[33:37], refs[37:]
    gm, n_ref, g_ref, work, score_sum, grad_small, halo_out, halo_in, rows_out, rows_in, page_rows, normed, cots = refs[0:13]
    acc, paired, slots, load_sem, misc_sem = refs[13:18]
    qkv, attn, attended, hidden, act, dgelu, x_ref = bufs
    wqkv, wproj, wfc1, wfc2 = weights
    gpre, dqkv = dgelu, qkv
    ex = Exchange(dp, acc, paired, slots, total, refs[18:23])
    core = ex.core
    tokens = g_ref.shape[0]
    low_masks, masks = head_masks(BF), head_masks(F32)
    def fetch(layer, names):
        for name in names:
            if name < 7:
                pltpu.make_async_copy(saved[layer][name], bufs[name], load_sem.at[layer, name]).start()
            else:
                i = name - 7

                @pl.when(core == layer)
                def _():
                    pltpu.make_async_copy(own[i], weights[i], load_sem.at[layer, name]).start()

                @pl.when(core != layer)
                def _():
                    pltpu.make_async_copy(other[i], weights[i], load_sem.at[layer, name]).start()

    def fetched(layer, *names):
        for name in names:
            target = bufs[name] if name < 7 else weights[name - 7]
            source = saved[0][name] if name < 7 else own[name - 7]
            pltpu.make_async_copy(source, target, load_sem.at[layer, name]).wait()

    def refill(step, names):
        @pl.when(step == 0)
        def _():
            fetch(0, names)

    fetch_order = [10, 5, 4, 3, 9, 2, 8, 0, 1, 7, 6]
    grad_copy = pltpu.make_async_copy(grad_own, g_ref, misc_sem.at[0])
    merge_copies = [pltpu.make_async_copy(normed_hbm, normed, misc_sem.at[6]), pltpu.make_async_copy(cots_hbm, cots, misc_sem.at[7])]
    for copy in merge_copies:
        copy.start()
    grad_copy.start()
    fetch(1, fetch_order)
    ex.greet()
    halo_copy = pltpu.make_async_remote_copy(
        src_ref=halo_out, dst_ref=halo_in, send_sem=misc_sem.at[1], recv_sem=misc_sem.at[2],
        device_id=(ex.partner, ex.me), device_id_type=MESH)
    rows_copy = pltpu.make_async_remote_copy(
        src_ref=rows_out, dst_ref=rows_in, send_sem=misc_sem.at[3], recv_sem=misc_sem.at[4],
        device_id=(ex.partner, ex.me), device_id_type=MESH)
    last_copy = pltpu.make_async_copy(page_rows, grad_x, misc_sem.at[5])
    pages = tokens // (2 * WP)

    def half_of(half):
        return pl.ds(pl.multiple_of(half * 256, 256), 256)

    def send_rows():
        rows_out[...] = g_ref[:, half_of(ex.partner)].astype(BF)
        rows_copy.start()

    def place_rows():
        rows_copy.wait()
        mine = g_ref[:, half_of(core)]
        high = mine.astype(BF)
        low = (mine - high.astype(F32)).astype(BF)
        for p in range(pages):
            rows = slice(p * 2 * WP, (p + 1) * 2 * WP)
            placed = (
                mm(place_back[core], high[rows]) + mm(place_back[core], low[rows]) + mm(place_back[ex.partner], rows_in[rows, :]))
            for r in range(PAGE):
                page_rows[p, r] = placed[r * PAGE : r * PAGE + PAGE]
        last_copy.start()


    def put(row, value):
        grad_small[row : row + 1] = jnp.sum(value, axis=0, keepdims=True)

    def fc2_piece(step, layer, half):
        vectors = small.at[layer]
        owner = core == layer
        if half == 0:
            grad_small[...] = jnp.zeros_like(grad_small)

            @pl.when(step == 0)
            def _():
                grad_copy.wait()

            @pl.when(step == 1)
            def _():
                halo_copy.wait()
                g_ref[...] = g_ref[...] + by_page_back(pages, send0, halo_in[...])

            gm[...] = g_ref[...].astype(BF)
            put(7, gm[...].astype(F32))
            fetched(layer, 10, 5)
        for j in range(half * 4, half * 4 + 4):
            cols = slice(j * 256, j * 256 + 256)
            low = (mm_nt(gm[...], wfc2[cols, :]) * dgelu[:, cols].astype(F32)).astype(BF)
            gpre[:, cols] = low
            grad_small[8 + j // 2 : 9 + j // 2, (j % 2) * 256 : (j % 2) * 256 + 256] = jnp.sum(
                low.astype(F32), axis=0, keepdims=True)
        if half == 0:
            fetched(layer, 4)
        for b in range(half * 2, half * 2 + 2):
            ex.emit(4 + b, owner, mm_tn(act[:, b * 512 : b * 512 + 512], gm[...]).astype(BF))
        if half == 1:
            refill(step, [4, 10])

    def fc1_piece(step, layer):
        fetched(layer, 3)
        unit, _ = unit_norm(hidden[...])
        n_ref[...] = (unit * small[layer, 5:6] + small[layer, 6:7]).astype(BF)
        for b in range(4):
            ex.emit(8 + b, core == layer, mm_tn(n_ref[...], gpre[:, b * 512 : b * 512 + 512]).astype(BF))

    def norm_two_piece(step, layer):
        fetched(layer, 9)
        for j in range(2):
            work[:, j * 256 : j * 256 + 256] = mm_nt(gpre[...], wfc1[j * 256 : j * 256 + 256, :])
        unit, inv_std = unit_norm(hidden[...])
        dn = work[...]
        put(5, dn * unit)
        put(6, dn)
        g_ref[...] = g_ref[...] + unit_norm_back(dn, unit, inv_std, small[layer, 5:6])
        gm[...] = g_ref[...].astype(BF)
        put(4, gm[...].astype(F32))
        refill(step, [5, 3, 9])

    def proj_piece(step, layer):
        fetched(layer, 2, 8)
        ex.emit(12, core == layer, mm_tn(attended[...], gm[...]).astype(BF))
        for j in range(2):
            n_ref[:, j * 256 : j * 256 + 256] = mm_nt(gm[...], wproj[j * 256 : j * 256 + 256, :]).astype(BF)
        score_sum[...] = jnp.zeros_like(score_sum)
        fetched(layer, 0, 1)
        refill(step, [2, 8])

    def window(w, carry):
        rows = aligned(w * WP, WP)
        for blk in range(4):
            cols = [slice(i * 512 + blk * 128, i * 512 + blk * 128 + 128) for i in range(3)]
            q, k, v = [qkv[rows, c] for c in cols]
            g = n_ref[rows, cols[0]]
            a = attn[aligned((w * 4 + blk) * 4 * WP, 4 * WP), :]
            p = mm_nt(stack_heads(g, low_masks), v)
            wide = a.astype(F32)
            ap = wide * p
            low = (ap - wide * jnp.sum(ap, axis=-1, keepdims=True)).astype(BF)
            score_sum[blk * 4 * WP : (blk + 1) * 4 * WP, :] += low.astype(F32)
            gt, qt = g.T, q.T
            dv = [mm(gt[h * 32 : h * 32 + 32], a[h * WP : (h + 1) * WP]) for h in range(4)]
            dk = [mm(qt[h * 32 : h * 32 + 32], low[h * WP : (h + 1) * WP]) * 32**-0.5 for h in range(4)]
            dqkv[rows, cols[2]] = jnp.concatenate(dv, axis=0).astype(BF).T
            dqkv[rows, cols[1]] = jnp.concatenate(dk, axis=0).astype(BF).T
            dqkv[rows, cols[0]] = (pick_heads(mm(low, k), masks) * 32**-0.5).astype(BF)
        return carry

    def attention_piece(step, layer, half):
        count = tokens // WP // 2
        lax.fori_loop(0, count, lambda i, carry: window(half * count + i, carry), 0, unroll=3)

        @pl.when(half == 1)
        def _():
            refill(step, [1])

    def qkv_piece(step, layer):
        fetched(layer, 6)
        unit, _ = unit_norm(x_ref[...].astype(F32))
        n_ref[...] = (unit * small[layer, 0:1] + small[layer, 1:2]).astype(BF)
        for b in range(3):
            ex.emit(13 + b, core == layer, mm_tn(n_ref[...], dqkv[:, b * 512 : b * 512 + 512]).astype(BF))
        put(2, dqkv[:, 0:512].astype(F32))
        put(3, dqkv[:, 1024:1536].astype(F32))

    def norm_one_piece(step, layer):
        fetched(layer, 7)
        for j in range(2):
            work[:, j * 256 : j * 256 + 256] = mm_nt(dqkv[...], wqkv[j * 256 : j * 256 + 256, :])
        unit, inv_std = unit_norm(x_ref[...].astype(F32))
        dn = work[...]
        put(0, dn * unit)
        put(1, dn)
        g_ref[...] = g_ref[...] + unit_norm_back(dn, unit, inv_std, small[layer, 0:1])

        @pl.when(step == 0)
        def _():
            gm[...] = g_ref[...].astype(BF)
            halo_out[...] = by_page_back(pages, halo1, gm[...]).astype(BF)
            halo_copy.start()
            g_ref[...] = by_page_back(pages, own1, gm[...])

        refill(step, [0, 7, 6])
        reduce_table(score_sum, select, back, grad_small.at[16:32])
        grad_small[32:40] = merge_sums[...]
        ex.emit(16, core == layer, jnp.concatenate([grad_small[...], jnp.zeros((UNIT - 48, 512), F32)], axis=0).astype(BF))

    pieces = [partial(fc2_piece, half=0), partial(fc2_piece, half=1), fc1_piece, norm_two_piece, proj_piece,
              attention_piece, None, qkv_piece, norm_one_piece]

    for copy in merge_copies:
        copy.wait()
    for half in range(2):
        for k in range(4):
            ex.emit(k, core == half, mm_tn(normed[:, k * 512 : k * 512 + 512], cots[half]).astype(BF))

    def tick(t, done):
        done = ex.tick(t, done)
        step, place = t // len(pieces), lax.rem(t, len(pieces))
        layer = 1 - step
        for i, piece in enumerate(pieces):
            if piece is attention_piece:
                @pl.when(jnp.logical_and(jnp.logical_or(place == i, place == i + 1), step < 2))
                def _():
                    attention_piece(step, layer, place - i)
            elif piece is not None:
                @pl.when(jnp.logical_and(place == i, step < 2))
                def _():
                    piece(step, layer)

        @pl.when(t == 2 * len(pieces))
        def _():
            send_rows()

        @pl.when(t == 2 * len(pieces) + 2)
        def _():
            place_rows()

        return done

    ticks = 1 + max(t for core in ex.table for chunk in core for t in chunk)
    lax.fori_loop(0, max(ticks, 2 * len(pieces) + 3), tick, [jnp.int32(0)] * (ex.steps + 1))
    ex.end()
    last_copy.wait()


def widen_kernel(total, page_rows, turn, wqkv, wproj, wfc1, wfc2, wmerge, pages_out, *refs):
    singles, (fc1_bias, merge_gain, merge_bias, table, rows, stage, passing, load_sem, store_sem, pass_sem) = refs[0:8], refs[8:]
    pass_in = pltpu.make_async_copy(page_rows, passing, pass_sem.at[0])
    pass_out = pltpu.make_async_copy(passing, pages_out, pass_sem.at[1])
    pass_in.start()
    blocks = [(b * 512, wmerge.at[b * 512 : b * 512 + 512, :]) for b in range(4)]
    blocks += [(2048 + b * 512, wfc2.at[b * 512 : b * 512 + 512, :]) for b in range(4)]
    blocks += [(4096 + b * 512, wfc1.at[:, b * 512 : b * 512 + 512]) for b in range(4)]
    blocks += [(6144, wproj)]
    blocks += [(6656 + b * 512, wqkv.at[:, b * 512 : b * 512 + 512]) for b in range(3)]
    loads = []
    for i, (start, _) in enumerate(blocks + [(8192, None)]):
        count = min(512, total.shape[0] - start)
        copy = pltpu.make_async_copy(total.at[start : start + count], rows.at[start : start + count], load_sem.at[i])
        copy.start()
        loads.append(copy)
    stores = []
    for i, (start, target) in enumerate(blocks):
        slot = i % 4
        loads[i].wait()
        if i == 1:
            pass_in.wait()
            pass_out.start()
        if i >= 4:
            stores[i - 4].wait()
        stage[slot] = rows[start : start + 512, :].astype(F32)
        copy = pltpu.make_async_copy(stage.at[slot], target, store_sem.at[slot])
        copy.start()
        stores.append(copy)
    loads[-1].wait()
    tail = rows[8192:8240, :].astype(F32)
    for k in range(8):
        singles[k][...] = tail[k : k + 1]
    for k in range(4):
        cols = slice(k * 512, k * 512 + 512)
        fc1_bias[:, cols] = tail[8 + k : 9 + k]
        merge_gain[:, cols] = tail[32 + k : 33 + k]
        merge_bias[:, cols] = tail[36 + k : 37 + k]
    high = rows[8208:8224, 0:384].astype(BF)
    table[...] = mm(high, turn[...])
    for copy in stores[-4:]:
        copy.wait()
    pass_out.wait()


HBM = pl.BlockSpec(memory_space=pl.ANY)
VMEM = pl.BlockSpec(memory_space=pltpu.VMEM)


def scratch_of(entry):
    if entry is None:
        return pltpu.SemaphoreType.DMA
    if isinstance(entry, int):
        return pltpu.SemaphoreType.DMA((entry,))
    if isinstance(entry[0], int):
        return pltpu.SemaphoreType.DMA(entry)
    return pltpu.VMEM(*entry)


def call(kernel, args, outs, scratch, name, collective_id=None):
    return pl.pallas_call(
        kernel,
        out_shape=[jax.ShapeDtypeStruct(s, d) for s, d, _ in outs],
        in_specs=[spec for _, spec in args],
        out_specs=[spec for _, _, spec in outs],
        scratch_shapes=[scratch_of(s) for s in scratch],
        compiler_params=pltpu.CompilerParams(
            vmem_limit_bytes=VMEM_LIMIT, collective_id=collective_id, has_side_effects=collective_id is not None),
        name=name,
    )(*[value for value, _ in args])


def shards(
    page_inputs, gain_one, bias_one, qkv_weight, query_bias, value_bias, bias_table, proj_weight, proj_bias,
    gain_two, bias_two, fc1_weight, fc1_bias, fc2_weight, fc2_bias, merge_gain, merge_bias, merge_weight, cotangent,
):
    dp = lax.axis_size("dp")
    pages = page_inputs.shape[0]
    tokens = pages * 2 * WP
    heads = bias_table.shape[2]
    table = bias_table.shape[1]
    place = place_tables(pages)
    select, back = code_matrices()
    merged_rows, cot_rows = place["pick"].shape[1:]

    turned = np.zeros((table, 384), np.float32)
    for u in range(table):
        turned[table - 1 - u, (u - 4) % 384] = 1
    params = [gain_one, bias_one, query_bias, value_bias, proj_bias, gain_two, bias_two, fc2_bias, fc1_bias,
              merge_gain.reshape(16, 128), merge_bias.reshape(16, 128), bias_table[0].T, jnp.asarray(turned, BF)]
    own = [qkv_weight[0], proj_weight[0], fc1_weight[0], fc2_weight[0]]
    xh = page_inputs.reshape(pages * 400, 256)
    cot = cotangent.transpose(1, 2, 0, 3)
    cot = jnp.pad(cot, ((0, 0), (0, 0), (0, cot_rows // AREA - pages), (0, 0))).reshape(cot_rows, 512)

    def at(spec, *values):
        return [(v, spec) for v in values]

    rows = ((tokens, 512), BF)
    wide_rows = ((tokens, 512), F32)
    saved_shapes = [((tokens, 1536), BF), ((pages * 2 * heads * WP, WP), BF), rows, wide_rows,
                    ((tokens, 2048), BF), ((tokens, 2048), BF)]
    weight_shapes = [(w.shape, BF) for w in own]
    halo = ((pages * WP, 512), BF)
    halos = ((3, pages * WP, 512), BF)
    parts_shape = ((2, 2048, 512), BF)
    mrows = (merged_rows, 512)
    results = call(
        forward_kernel,
        at(HBM, xh, cot) + at(VMEM, *params, window_masks(),
                                    *[place[n] for n in ("take", "pick", "send0", "own1", "halo1", "own2", "halo2")], select)
        + at(HBM, *own, merge_weight),
        [(*shape, HBM) for shape in (saved_shapes + [rows]) * 2 + weight_shapes]
        + [((cot_rows, 512), BF, VMEM), ((merged_rows, 2048), BF, VMEM), ((2, *mrows), BF, VMEM), ((8, 512), F32, VMEM), ((2, 16, 512), F32, VMEM), (*wide_rows, VMEM)],
        weight_shapes * 2 + [parts_shape] + saved_shapes
        + [rows, rows, ((heads * WP, WP), BF), ((2, *xh.shape), BF), ((2, 32, 512), BF), ((2, cot_rows, 512), BF), rows, halos, halos,
           ((merged_rows, 2048), F32), ((merged_rows, 2048), F32), ((2, *mrows), BF), (mrows, BF),
           8, (2, 7), 4, 12, 12],
        "forward", collective_id=1)
    saved0, saved1, other = results[0:7], results[7:14], results[14:18]
    merged, normed, cots, merge_sums, small, grad_own = results[18:]

    chunks, units = ROWS // CHUNK, ROWS // UNIT
    page_half = ((pages, PAGE, PAGE, 256), F32)
    total, grad_pages = call(
        partial(backward_kernel, dp),
        at(HBM, grad_own) + at(VMEM, place["own1"], place["halo1"], place["send0"], place["back"], small, select, back, merge_sums)
        + at(HBM, *saved0, *saved1, *own, *other, normed, cots),
        [((ROWS, 512), BF, HBM), (*page_half, HBM)],
        saved_shapes + [rows] + weight_shapes
        + [rows, rows, wide_rows, wide_rows, ((heads * WP, WP), F32), ((48, 512), F32), halo, halo,
           ((tokens, 256), BF), ((tokens, 256), BF), page_half, ((merged_rows, 2048), BF), ((2, *mrows), BF)]
        + [((ROWS + RING * 512, 512), BF), ((ROWS, 512), BF), ((chunks * SLOT, 512), BF), (2, 11), 8,
           units, units, chunks, (chunks, STEPS), (chunks, STEPS)],
        "backward", collective_id=0)
    if dp != CHIPS:
        total = lax.psum(total.astype(F32), "dp")

    turn = np.zeros((384, table), np.float32)
    for u in range(table):
        turn[u + 3, table - 1 - u] = 1
    wide_row = ((1, 2048), F32, VMEM)
    g_qkv, g_proj, g_fc1, g_fc2, g_merge, grad_pages, *single, g_fc1_bias, g_gain, g_bias, g_table = call(
        widen_kernel, at(HBM, total, grad_pages) + at(VMEM, jnp.asarray(turn, BF)),
        [((512, 1536), F32, HBM), ((512, 512), F32, HBM), ((512, 2048), F32, HBM), ((2048, 512), F32, HBM),
         ((2048, 512), F32, HBM), (*page_half, HBM)] + [((1, 512), F32, VMEM)] * 8
        + [wide_row, wide_row, wide_row, ((heads, table), F32, VMEM)],
        [((ROWS, 512), total.dtype), ((4, 512, 512), F32), page_half, 17, 4, 2], "widen")
    merged = merged.reshape(10, 10, cot_rows // AREA, 512)[:, :, :pages].transpose(2, 0, 1, 3)
    return (
        merged, grad_pages,
        single[0], single[1], g_qkv[None], single[2], single[3], g_table.T[None], g_proj[None], single[4], single[5], single[6],
        g_fc1[None], g_fc1_bias, g_fc2[None], single[7], g_gain.reshape(2048), g_bias.reshape(2048), g_merge,
    )


def solution(mesh):
    row, mat = P("pipe", None), P("pipe", None, None)
    wide = P("dp", None, None, "pipe")
    in_specs = (wide, row, row, mat, row, row, mat, mat, row, row, row, mat, row, mat, row, P(), P(), P(None, "pipe"), wide)
    out_specs = (wide, wide, row, row, mat, row, row, mat, mat, row, row, row, mat, row, mat, row, P(), P(), P(None, "pipe"))
    return jax.shard_map(shards, mesh=mesh, in_specs=in_specs, out_specs=out_specs, check_vma=False)
```

time: 327 us -> 222 us (0.68)
  Pallas kernels: 277 us -> 213 us
  local copies, waits for them, and re-layouts: 27.6 us -> 5.03 us
  other arithmetic: 6.42 us -> 0 us
  starting transfers between devices: 4.65 us -> 0 us
  waiting for transfers between devices: 4.61 us -> 0 us
    pallas_call x1 -> x0, Pallas kernels: 152 us -> none  [sum_rows(): pl.pallas_call(functools.partial(comm_kernel, dp, count, chunk), out_shap...]
    pallas_call x6 -> x3, Pallas kernels: 125 us -> 213 us  [call(): pl.pallas_call(kernel, out_shape=[jax.ShapeDtypeStruct(s, d) for s, d, _...]
    unnamed x29 -> x2, local copies, waits for them, and re-layouts: 12.6 us -> 0.01 us
    slice x8 -> x0, local copies, waits for them, and re-layouts: 4.73 us -> none  [the longest x1 1.62 us: shards(): tail[7:8]]
    ppermute x15 -> x0, starting transfers between devices: 4.65 us -> none  [other_core(): return lax.ppermute(value, 'pipe', [(0, 1), (1, 0)])]
    ppermute x15 -> x0, waiting for transfers between devices: 4.61 us -> none  [other_core(): return lax.ppermute(value, 'pipe', [(0, 1), (1, 0)])]
    dynamic_slice x6 -> x0, local copies, waits for them, and re-layouts: 3.71 us -> none  [the longest x1 1.69 us: shards(): lax.dynamic_slice_in_dim(cotangent, (1 - core) * 5, 5, axis=1)]
  transfers between devices with their start and end apart: 15 -> 0, of which waited for: 7 -> 0; matrix products, arithmetic and copies ran while one was open for 7% -> 0% of each run, Pallas kernels for 12% -> 0%
where the time goes in v2:
time: 222 us; the launch traced here: 219 us
  Pallas kernels  213 us (96%)
  local copies, waits for them, and re-layouts  5.03 us (2%)
    pallas_call x3, Pallas kernels, call(): pl.pallas_call(kernel, out_shape=[jax.ShapeDtypeStruct(s, d) for s, d, _...  213 us

profile of v2, /device:TPU:0, one launch (start us, length us, event | category | flops | bytes accessed | tf_op | source)
XLA Modules:
  0.0 218.5 jit_solution(6599457952002097765)
XLA Ops:
  0.7 0.0 copy-start
  0.7 1.2 pad.4
  1.9 0.8 reshape.60.cot
  2.8 0.0 copy-done
  2.8 0.9 reshape.59.xh
  3.7 42.2 %forward.1 = (bf16[672,1536]{1,0:T(8,128)(2,1)}, bf16[10752,112]{1,0:T(8,128)(2,1)}, bf16[672,512]{1,0:T(8,128)(2,1)}, f32[672,512]{1,0:T(8,128)}, bf16[672,2048...) custom-call(bf16[1200,256]{1,0:T(8,128)(2,1)} %reshape.59.xh, ...), custom_call_target="tpu_custom_call" | custom-call | tf_op jit(solution)/shard_map/forward/pallas_call | solution.py:878
  45.9 1.1 reshape.63
  47.0 0.9 slice_bitcast_fusion
  47.9 158.3 %backward.1 = (bf16[8448,512]{1,0:T(8,128)(2,1)}, f32[3,20,20,256]{3,2,1,0:T(8,128)}) custom-call(f32[672,512]{1,0:T(8,128)} %get-tuple-element.64.grad_own, bf16[224,224]{1,0:T(8,128)(2,1)} %constant.33.clone.own1, bf16[224,112]{1,0:T(8,128)(2,1)} %constant.34.clone.halo1, bf16[112,224]{1,0:T(8,128)(2,1)} %constant.32.clone.send0, ...), custom_call_target="tpu_custom_call" | custom-call | tf_op jit(solution)/shard_map/backward/pallas_call | solution.py:878
  206.2 12.1 %widen.1 = (f32[512,1536]{1,0:T(8,128)}, f32[512,512]{1,0:T(8,128)}, f32[512,2048]{1,0:T(8,128)}, f32[2048,512]{1,0:T(8,128)}, f32[2048,512]{1,0:T(8,128)}, /*in...) custom-call(bf16[8448,512]{1,0:T(8,128)(2,1)} %get-tuple-element.87., ...), custom_call_target="tpu_custom_call" | custom-call | tf_op jit(solution)/shard_map/widen/pallas_call | solution.py:878
Async XLA Ops:
  0.7 2.1 copy-start

commit v3 on v2

--- a/solution.py
+++ b/solution.py
@@ -28,8 +28,8 @@
 EMITS = [(r, r + 512) for r in range(0, 8192, 512)] + [(8192, 8448)]
 KINDS = (0, 2, 0, 1, 1, 3, 1, 0, 0, 1, 2)
 SCHEDULE = (
-    ((1, 3, 6, 8, 9, 10, 12, 15, 17), (1, 3, 6, 8, 9, 10, 12, 15, 17), (14, 16, 18, 21, 23, 30, 36, 46, 56), (14, 16, 18, 22, 28, 32, 38, 46, 56), (15, 17, 19, 25, 31, 35, 44, 53, 59), (16, 21, 27, 34, 37, 41, 48, 55, 61), (16, 21, 27, 34, 37, 42, 50, 57, 63), (16, 21, 27, 34, 39, 45, 51, 57, 63), (20, 26, 33, 38, 43, 49, 54, 60, 64), (20, 26, 33, 40, 47, 52, 58, 62, 65), (24, 29, 36, 40, 47, 52, 58, 62, 66)),
-    ((1, 4, 6, 7, 8, 9, 10, 12, 16), (1, 4, 6, 7, 8, 9, 10, 12, 16), (2, 5, 7, 9, 10, 13, 16, 18, 23), (2, 5, 7, 9, 10, 13, 16, 18, 23), (3, 6, 8, 9, 10, 13, 17, 18, 25), (4, 6, 8, 9, 10, 13, 17, 20, 28), (4, 7, 9, 10, 14, 16, 18, 24, 31), (4, 7, 9, 11, 14, 16, 19, 29, 31), (9, 11, 14, 17, 18, 21, 30, 34, 38), (9, 11, 14, 18, 22, 27, 33, 36, 39), (10, 13, 17, 18, 26, 32, 35, 37, 40)),
+    ((1, 3, 6, 8, 9, 10, 12, 15, 17), (1, 3, 6, 8, 9, 10, 12, 15, 17), (14, 16, 18, 21, 23, 30, 36, 46, 52), (14, 16, 18, 22, 28, 32, 38, 46, 52), (15, 17, 19, 25, 31, 35, 44, 49, 54), (16, 21, 27, 34, 37, 41, 48, 51, 56), (16, 21, 27, 34, 37, 42, 48, 53, 57), (16, 21, 27, 34, 39, 45, 48, 53, 57), (20, 26, 33, 38, 43, 47, 50, 55, 58), (20, 26, 33, 38, 44, 47, 51, 55, 58), (24, 29, 36, 38, 44, 47, 51, 55, 58)),
+    ((2, 4, 6, 7, 8, 9, 10, 12, 16), (2, 4, 6, 7, 8, 9, 10, 12, 16), (2, 5, 7, 9, 10, 13, 16, 18, 23), (2, 5, 7, 9, 10, 13, 16, 18, 23), (3, 6, 8, 9, 10, 13, 17, 18, 25), (4, 6, 8, 9, 10, 13, 17, 20, 28), (4, 7, 9, 10, 14, 16, 18, 24, 31), (4, 7, 9, 11, 14, 16, 19, 29, 31), (9, 11, 14, 17, 18, 21, 30, 34, 38), (9, 11, 14, 18, 22, 27, 33, 36, 39), (10, 13, 17, 18, 26, 32, 35, 37, 40)),
 )
 FALLBACK = (((19,),) * 11, ((19,),) * 11)
 
@@ -100,7 +100,8 @@
                     else:
                         halo2[row, p * WP + r * PAGE + col] = 1
     return {name: jnp.asarray(t, BF) for name, t in dict(
-        take=take, back=take.transpose(0, 2, 1), pick=pick, send0=send0, own1=own1, halo1=halo1, own2=own2, halo2=halo2).items()}
+        take=take, back=take.transpose(0, 2, 1), pick=pick, send0=send0, own1=own1, halo1=halo1, own2=own2, halo2=halo2,
+        own2_back=own2.T, halo2_back=halo2.T).items()}
 
 
 def window_masks():
@@ -231,14 +232,14 @@
         out[:, cols] = (hidden[:, cols] + (mm(act[...], weights[3][:, cols]) + small[7:8, cols])).astype(BF)
 
 
-def forward_kernel(xh, cot, gain_one, bias_one, query_bias, value_bias, proj_bias, gain_two, bias_two, fc2_bias, fc1_bias,
-                   merge_gain, merge_bias, table, turned, masks, take, pick, send0, own1, halo1, own2, halo2, select, *refs):
+def forward_kernel(page_places, cot_places, gain_one, bias_one, query_bias, value_bias, proj_bias, gain_two, bias_two, fc2_bias, fc1_bias,
+                   merge_gain, merge_bias, table, turned, masks, take, pick, send0, own1, halo1, own2, halo2, select, own2_turned, halo2_turned, *refs):
     own, saved, other = refs[0:5], (refs[5:12], refs[12:19]), refs[19:23]
-    merged, normed, grad_cots, merge_sums, small, grad = refs[23:29]
+    merged, normed_out, cots_out, merge_sums, small, grad = refs[23:29]
     weights, wm, bufs = (refs[29:33], refs[33:37]), refs[37], refs[38:44]
     x_ref, n_ref, pos, rows_in, pack_in, cots, out, halo_out, halo_in = refs[44:53]
-    rows_ref, ghead, msel, mrecv = refs[53:57]
-    load_sem, keep_sem, other_sem, send_sem, recv_sem = refs[57:62]
+    rows_ref, ghead, msel, mrecv, cot_wide, page_wide, normed, grad_cots, own2_back, halo2_back = refs[53:63]
+    load_sem, keep_sem, other_sem, send_sem, recv_sem, misc_sem = refs[63:69]
     core, me = lax.axis_index("pipe"), lax.axis_index("dp")
     partner = 1 - core
     pages = x_ref.shape[0] // (2 * WP)
@@ -248,7 +249,7 @@
             src_ref=source, dst_ref=target, send_sem=send_sem.at[i], recv_sem=recv_sem.at[i],
             device_id=(partner, me), device_id_type=MESH)
 
-    shared = [(xh, rows_in), (pack_in.at[core], pack_in), (cot, cots), (own[4], wm)]
+    shared = [(rows_in.at[core], rows_in), (pack_in.at[core], pack_in), (cots.at[core], cots), (own[4], wm)]
     local = [pltpu.make_async_copy(source, target.at[core], load_sem.at[4 + i]) for i, (source, target) in enumerate(shared)]
     sends = [remote(4 + i, source, target.at[core]) for i, (source, target) in enumerate(shared)]
     gets = [remote(4 + i, source, target.at[partner]) for i, (source, target) in enumerate(shared)]
@@ -265,15 +266,22 @@
             def _():
                 action(layer)
 
-    local[0].start()
 
     def load(layer):
         for i in range(4):
             loading(layer, i).start()
 
     each_core(load)
-    local[2].start()
     local[3].start()
+    late = [pltpu.make_async_copy(own2_turned, own2_back, misc_sem.at[0]), pltpu.make_async_copy(halo2_turned, halo2_back, misc_sem.at[1])]
+    for copy in late:
+        copy.start()
+    early = [pltpu.make_async_copy(normed, normed_out, misc_sem.at[2]), pltpu.make_async_copy(grad_cots, cots_out, misc_sem.at[3])]
+    for p in range(pages):
+        for r in range(PAGE):
+            row = (p * PAGE + r) * PAGE
+            page_wide[row : row + PAGE, :] = page_places[p, r].astype(F32)
+    rows_in[core] = page_wide[...].astype(BF)
     singles = [gain_one, bias_one, query_bias, value_bias, proj_bias, gain_two, bias_two, fc2_bias]
     rows = [row[...].astype(F32) for row in singles] + [fc1_bias[:, k * 512 : k * 512 + 512].astype(F32) for k in range(4)]
     pack_in[core, 0:16, :] = jnp.concatenate(rows + [jnp.zeros((4, 512), F32)], axis=0).astype(BF)
@@ -290,6 +298,11 @@
             pushing(layer, i).start()
 
     each_core(push)
+    cot_wide[...] = jnp.zeros_like(cot_wide)
+    group = cot_wide.shape[0] // AREA
+    for place in range(AREA):
+        cot_wide[place * group : place * group + pages, :] = cot_places[place // 10, place % 10].astype(F32)
+    cots[core] = cot_wide[...].astype(BF)
     sends[2].start()
     sends[3].start()
 
@@ -313,7 +326,6 @@
     gets[1].wait_recv()
     small[...] = pack_in[:, 0:16, :].astype(F32)
     expand_table(pack_in.at[0, 16:32, 0:384], select, pos)
-    local[0].wait()
     gets[0].wait_recv()
     for half in range(2):
         for p in range(pages):
@@ -339,7 +351,6 @@
     halo[1].start()
 
     count = rows_ref.shape[0]
-    local[2].wait()
     gets[2].wait_recv()
     for half in range(2):
         grad_cots[half] = mm(pick[core], cots[half]).astype(BF)
@@ -352,6 +363,8 @@
     unit, inv_std = unit_norm(rows_ref[...])
     scale, shift = [jnp.concatenate([v[i : i + 1].astype(F32) for i in range(16)], axis=1) for v in (merge_gain[...], merge_bias[...])]
     normed[...] = (unit * scale + shift).astype(BF)
+    for copy in early:
+        copy.start()
     local[3].wait()
     gets[3].wait_recv()
     for half in range(2):
@@ -366,9 +379,11 @@
             merge_sums[i * 4 + k : i * 4 + k + 1] = over_rows[i][:, k * 512 : k * 512 + 512]
     grad_rows = unit_norm_back(grad_head, unit, inv_std, scale).astype(BF)
     stacked = jnp.concatenate([grad_rows[:, k * 512 : k * 512 + 512] for k in range(4)], axis=0)
-    halo_out[2] = mm_tn(halo2[...], stacked).astype(BF)
+    for copy in late:
+        copy.wait()
+    halo_out[2] = mm(halo2_back[...], stacked).astype(BF)
     halo[2].start()
-    grad[...] = mm_tn(own2[...], stacked)
+    grad[...] = mm(own2_back[...], stacked)
     for half in range(2):
         msel[half] = mm(normed[...], wm[half]).astype(BF)
     rows_copy = remote(11, msel.at[partner], mrecv)
@@ -380,6 +395,8 @@
 
     for copy in sends + halo + [rows_copy]:
         copy.wait_send()
+    for copy in early:
+        copy.wait()
     for i in range(7):
         kept(1, i).wait()
 
@@ -815,8 +832,8 @@
     last_copy.wait()
 
 
-def widen_kernel(total, page_rows, turn, wqkv, wproj, wfc1, wfc2, wmerge, pages_out, *refs):
-    singles, (fc1_bias, merge_gain, merge_bias, table, rows, stage, passing, load_sem, store_sem, pass_sem) = refs[0:8], refs[8:]
+def widen_kernel(total, page_rows, merged_rows, turn, wqkv, wproj, wfc1, wfc2, wmerge, pages_out, *refs):
+    singles, (fc1_bias, merge_gain, merge_bias, table, merged, rows, stage, passing, wide, load_sem, store_sem, pass_sem) = refs[0:8], refs[8:]
     pass_in = pltpu.make_async_copy(page_rows, passing, pass_sem.at[0])
     pass_out = pltpu.make_async_copy(passing, pages_out, pass_sem.at[1])
     pass_in.start()
@@ -844,6 +861,10 @@
         copy = pltpu.make_async_copy(stage.at[slot], target, store_sem.at[slot])
         copy.start()
         stores.append(copy)
+    wide[...] = merged_rows[...].astype(F32)
+    group = wide.shape[0] // AREA
+    for place in range(AREA):
+        merged[place // 10, place % 10] = wide[place * group : place * group + merged.shape[2], :].astype(BF)
     loads[-1].wait()
     tail = rows[8192:8240, :].astype(F32)
     for k in range(8):
@@ -906,9 +927,6 @@
     params = [gain_one, bias_one, query_bias, value_bias, proj_bias, gain_two, bias_two, fc2_bias, fc1_bias,
               merge_gain.reshape(16, 128), merge_bias.reshape(16, 128), bias_table[0].T, jnp.asarray(turned, BF)]
     own = [qkv_weight[0], proj_weight[0], fc1_weight[0], fc2_weight[0]]
-    xh = page_inputs.reshape(pages * 400, 256)
-    cot = cotangent.transpose(1, 2, 0, 3)
-    cot = jnp.pad(cot, ((0, 0), (0, 0), (0, cot_rows // AREA - pages), (0, 0))).reshape(cot_rows, 512)
 
     def at(spec, *values):
         return [(v, spec) for v in values]
@@ -924,15 +942,16 @@
     mrows = (merged_rows, 512)
     results = call(
         forward_kernel,
-        at(HBM, xh, cot) + at(VMEM, *params, window_masks(),
+        at(VMEM, page_inputs, cotangent.transpose(1, 2, 0, 3), *params, window_masks(),
                                     *[place[n] for n in ("take", "pick", "send0", "own1", "halo1", "own2", "halo2")], select)
-        + at(HBM, *own, merge_weight),
+        + at(HBM, place["own2_back"], place["halo2_back"]) + at(HBM, *own, merge_weight),
         [(*shape, HBM) for shape in (saved_shapes + [rows]) * 2 + weight_shapes]
-        + [((cot_rows, 512), BF, VMEM), ((merged_rows, 2048), BF, VMEM), ((2, *mrows), BF, VMEM), ((8, 512), F32, VMEM), ((2, 16, 512), F32, VMEM), (*wide_rows, VMEM)],
+        + [((cot_rows, 512), BF, VMEM), ((merged_rows, 2048), BF, HBM), ((2, *mrows), BF, HBM), ((8, 512), F32, VMEM), ((2, 16, 512), F32, VMEM), (*wide_rows, VMEM)],
         weight_shapes * 2 + [parts_shape] + saved_shapes
-        + [rows, rows, ((heads * WP, WP), BF), ((2, *xh.shape), BF), ((2, 32, 512), BF), ((2, cot_rows, 512), BF), rows, halos, halos,
-           ((merged_rows, 2048), F32), ((merged_rows, 2048), F32), ((2, *mrows), BF), (mrows, BF),
-           8, (2, 7), 4, 12, 12],
+        + [rows, rows, ((heads * WP, WP), BF), ((2, pages * 400, 256), BF), ((2, 32, 512), BF), ((2, cot_rows, 512), BF), rows, halos, halos,
+           ((merged_rows, 2048), F32), ((merged_rows, 2048), F32), ((2, *mrows), BF), (mrows, BF), ((cot_rows, 512), F32), ((pages * 400, 256), F32),
+           ((merged_rows, 2048), BF), ((2, *mrows), BF), ((tokens, 4 * merged_rows), BF), ((pages * WP, 4 * merged_rows), BF),
+           8, (2, 7), 4, 12, 12, 4],
         "forward", collective_id=1)
     saved0, saved1, other = results[0:7], results[7:14], results[14:18]
     merged, normed, cots, merge_sums, small, grad_own = results[18:]
@@ -957,15 +976,14 @@
     for u in range(table):
         turn[u + 3, table - 1 - u] = 1
     wide_row = ((1, 2048), F32, VMEM)
-    g_qkv, g_proj, g_fc1, g_fc2, g_merge, grad_pages, *single, g_fc1_bias, g_gain, g_bias, g_table = call(
-        widen_kernel, at(HBM, total, grad_pages) + at(VMEM, jnp.asarray(turn, BF)),
+    g_qkv, g_proj, g_fc1, g_fc2, g_merge, grad_pages, *single, g_fc1_bias, g_gain, g_bias, g_table, merged = call(
+        widen_kernel, at(HBM, total, grad_pages) + at(VMEM, merged, jnp.asarray(turn, BF)),
         [((512, 1536), F32, HBM), ((512, 512), F32, HBM), ((512, 2048), F32, HBM), ((2048, 512), F32, HBM),
          ((2048, 512), F32, HBM), (*page_half, HBM)] + [((1, 512), F32, VMEM)] * 8
-        + [wide_row, wide_row, wide_row, ((heads, table), F32, VMEM)],
-        [((ROWS, 512), total.dtype), ((4, 512, 512), F32), page_half, 17, 4, 2], "widen")
-    merged = merged.reshape(10, 10, cot_rows // AREA, 512)[:, :, :pages].transpose(2, 0, 1, 3)
+        + [wide_row, wide_row, wide_row, ((heads, table), F32, VMEM), ((10, 10, pages, 512), BF, VMEM)],
+        [((ROWS, 512), total.dtype), ((4, 512, 512), F32), page_half, ((cot_rows, 512), F32), 17, 4, 2], "widen")
     return (
-        merged, grad_pages,
+        merged.transpose(2, 0, 1, 3), grad_pages,
         single[0], single[1], g_qkv[None], single[2], single[3], g_table.T[None], g_proj[None], single[4], single[5], single[6],
         g_fc1[None], g_fc1_bias, g_fc2[None], single[7], g_gain.reshape(2048), g_bias.reshape(2048), g_merge,
     )

time: 222 us -> 215 us (0.968)
  local copies, waits for them, and re-layouts: 5.03 us -> 0 us
  Pallas kernels: 213 us -> 210 us
    reshape x3 -> x0, local copies, waits for them, and re-layouts: 2.89 us -> none  [the longest x1 1.1 us: shards(): merged.reshape(10, 10, cot_rows // AREA, 512)[:, :, :pages]]
where the time goes in v3:
time: 215 us; the launch traced here: 211 us
  Pallas kernels  210 us (98%)
    pallas_call x3, Pallas kernels, call(): pl.pallas_call(kernel, out_shape=[jax.ShapeDtypeStruct(s, d) for s, d, _...  210 us

profile of v3, /device:TPU:0, one launch (start us, length us, event | category | flops | bytes accessed | tf_op | source)
XLA Modules:
  0.0 211.3 jit_solution(12283539159740913513)
XLA Ops:
  0.7 43.1 %forward.1 = (bf16[672,1536]{1,0:T(8,128)(2,1)}, bf16[10752,112]{1,0:T(8,128)(2,1)}, bf16[672,512]{1,0:T(8,128)(2,1)}, f32[672,512]{1,0:T(8,128)}, bf16[672,2048...) custom-call(bf16[3,20,20,256]{3,2,1,0:T(8,128)(2,1)} %page_places.1,, ...), custom_call_target="tpu_custom_call" | custom-call | tf_op jit(solution)/shard_map/forward/pallas_call | solution.py:899
  43.7 155.0 %backward.1 = (bf16[8448,512]{1,0:T(8,128)(2,1)}, f32[3,20,20,256]{3,2,1,0:T(8,128)}) custom-call(f32[672,512]{1,0:T(8,128)} %get-tuple-element.64.grad_own, bf16[224,224]{1,0:T(8,128)(2,1)} %constant.34.clone.own1, bf16[224,112]{1,0:T(8,128)(2,1)} %constant.35.clone.halo1, bf16[112,224]{1,0:T(8,128)(2,1)} %constant.33.clone.send0, ...), custom_call_target="tpu_custom_call" | custom-call | tf_op jit(solution)/shard_map/backward/pallas_call | solution.py:899
  198.7 12.4 %widen.1 = (f32[512,1536]{1,0:T(8,128)}, f32[512,512]{1,0:T(8,128)}, f32[512,2048]{1,0:T(8,128)}, f32[2048,512]{1,0:T(8,128)}, f32[2048,512]{1,0:T(8,128)}, /*in...) custom-call(bf16[8448,512]{1,0:T(8,128)(2,1)} %get-tuple-element.87., ...), custom_call_target="tpu_custom_call" | custom-call | tf_op jit(solution)/shard_map/widen/pallas_call | solution.py:899
